TPU v7x, 32 devices: a whole 2x2x4 slice. The times are simulated.
32 devices in a mesh: ctx: 8 (over z, y), head: 4 (over x, core).
Axes of the slice: x: 2, y: 2, z: 4, core: 2. Of those that a mesh axis runs over, the one named last changes fastest.
Arguments:
- tokens: bfloat16 [2, 1024, 4096], P(None, 'ctx', 'head'), may hold values from -6 to 6
- w_query: bfloat16 [4096, 2048], P('ctx', 'head'), may hold values from -0.09375 to 0.09375
- w_key: bfloat16 [4096, 2048], P('ctx', 'head'), may hold values from -0.09375 to 0.09375
- w_value: bfloat16 [4096, 2048], P('ctx', 'head'), may hold values from -0.09375 to 0.09375
- norm_gain: float32 [2048], P('head'), may hold values from 0.1 to 1.9
Outputs:
- attended: bfloat16 [2, 1024, 2048], P(None, 'ctx', 'head')
All inputs are finite; a program needn't handle non-finite values.
Results may differ from a plain program's by a relative error of at most 0.0072.
Values may be sent and summed in bfloat16 or wider, within the bound.
A program may use at most 192 MiB of HBM per device.

v0:
```python
import jax
import jax.numpy as jnp
from jax import lax
from jax.sharding import PartitionSpec as P

HD = 128


def entering(part, axis, combine, identity):
    place = lax.axis_index(axis)
    gathered = lax.all_gather(part, axis)
    state = jnp.zeros_like(part) + jnp.asarray(identity, part.dtype)

    def one(hop, state):
        return combine(state, lax.dynamic_index_in_dim(gathered, hop, 0, False))

    return lax.fori_loop(0, place, one, state)


def add_states(earlier, later):
    return earlier + later


def body(tokens, w_query, w_key, w_value, norm_gain):
    gathered = lax.all_gather(tokens, "head", axis=2, tiled=True)
    seq_count, span_len, model_dim = gathered.shape
    token_rows = gathered.reshape(seq_count * span_len, model_dim)
    features = w_query.shape[1]
    query_full = lax.all_gather(w_query, "ctx", axis=0, tiled=True)
    query_sum = jnp.dot(token_rows, query_full, preferred_element_type=jnp.float32)
    key_full = lax.all_gather(w_key, "ctx", axis=0, tiled=True)
    key_sum = jnp.dot(token_rows, key_full, preferred_element_type=jnp.float32)
    value_full = lax.all_gather(w_value, "ctx", axis=0, tiled=True)
    value_sum = jnp.dot(token_rows, value_full, preferred_element_type=jnp.float32)
    head_count = features // HD

    def heads_first(projected):
        shaped = projected.astype(jnp.bfloat16).reshape(seq_count, span_len, head_count, HD)
        return shaped.transpose(0, 2, 1, 3)

    query = heads_first(jax.nn.silu(query_sum))
    key_all = heads_first(jax.nn.silu(key_sum))
    value_all = heads_first(value_sum)
    positions = jnp.arange(span_len)
    causal = positions[:, None] >= positions[None, :]
    scores = jnp.einsum("shtd,shud->shtu", query, key_all, preferred_element_type=jnp.float32)
    masked = jnp.where(causal, scores, 0.0).astype(jnp.bfloat16)
    local_out = jnp.einsum("shtu,shud->shtd", masked, value_all, preferred_element_type=jnp.float32)
    states = jnp.einsum("shud,shue->shde", key_all, value_all, preferred_element_type=jnp.float32)
    prefix = entering(states, "ctx", add_states, jnp.zeros_like(states))
    from_prefix = jnp.einsum(
        "shtd,shde->shte", query, prefix.astype(jnp.bfloat16), preferred_element_type=jnp.float32
    )
    total = local_out + from_prefix
    scale_inv = lax.rsqrt(jnp.mean(total * total, axis=-1, keepdims=True) + 1e-06)
    gain_view = norm_gain.reshape(1, head_count, 1, HD)
    normed = total * scale_inv * gain_view
    return normed.transpose(0, 2, 1, 3).reshape(seq_count, span_len, features).astype(jnp.bfloat16)


def solution(mesh):
    in_specs = (
        P(None, "ctx", "head"),
        P("ctx", "head"),
        P("ctx", "head"),
        P("ctx", "head"),
        P("head"),
    )
    out_specs = P(None, "ctx", "head")
    return jax.shard_map(body, mesh=mesh, in_specs=in_specs, out_specs=out_specs, check_vma=False)
```

profile of v0, /device:TPU:0, one launch (start us, length us, event | category | flops | bytes accessed | tf_op | source)
XLA Modules:
  0.0 339.2 jit_solution(12180585524790085105)
XLA Ops:
  6.5 0.0 all-gather.7.cloned.1.call-start
  6.5 0.7 all-gather.7.cloned.1.call-update
  7.3 0.0 all-gather.11.cloned.1.call-start
  7.3 0.7 all-gather.11.cloned.1.call-update
  8.0 0.0 all-gather.13.cloned.1.call-start
  8.1 0.7 all-gather.13.cloned.1.call-update
  8.7 0.0 all-gather.9.cloned.1.call-start
  8.8 0.5 all-gather.9.cloned.1.call-update
  9.3 0.0 all-gather.15.cloned.1.call-start
  9.4 24.9 %all-gather.7.cloned.1.call-done = bf16[2,128,4096]{2,1,0:T(8,128)(2,1)} async-done(((bf16[2,128,1024]{2,1,0:T(8,128)(2,1)}), bf16[2,128,4096]{2,1,0:T(8,128)(2,1)}) %all-gather.7.cloned.1.call-update) | async-done | bytes 2097168 | tf_op jit(solution)/shard_map/all_gather | solution.py:25
  34.2 75.6 %all-gather.11.cloned.1.call-done = bf16[4096,512]{1,0:T(8,128)(2,1)} async-done(((bf16[512,512]{1,0:T(8,128)(2,1)}), bf16[4096,512]{1,0:T(8,128)(2,1)}) %all-gather.11.cloned.1.call-update) | async-done | bytes 4194320 | tf_op jit(solution)/shard_map/all_gather | solution.py:31
  109.8 0.0 copy-start.1
  109.8 4.3 %multiply_convert_fusion = bf16[256,512]{1,0:T(8,128)(2,1)S(1)} fusion(bf16[256,4096]{1,0:T(8,128)(2,1)} %bitcast.46, bf16[4096,512]{1,0:T(8,128)(2,1)} %all-gather.11.cloned.1.call-done), kind=kOutput, calls=%fused_computation.10 | convolution fusion | flops 1074397184 | bytes 6553600 | tf_op jit(solution)/shard_map/dot_general | solution.py:32
  114.1 0.1 reshape.26
  114.2 0.2 copy.13
  114.4 69.3 %all-gather.13.cloned.1.call-done = bf16[4096,512]{1,0:T(8,128)(2,1)} async-done(((bf16[512,512]{1,0:T(8,128)(2,1)}), bf16[4096,512]{1,0:T(8,128)(2,1)}) %all-gather.13.cloned.1.call-update) | async-done | bytes 4194320 | tf_op jit(solution)/shard_map/all_gather | solution.py:33
  183.6 0.0 copy-done.1
  183.6 3.4 %convolution_convert_fusion = bf16[256,512]{1,0:T(8,128)(2,1)S(1)} fusion(bf16[256,4096]{1,0:T(8,128)(2,1)S(1)} %bitcast.47, bf16[4096,512]{1,0:T(8,128)(2,1)} %all-gather.13.cloned.1.call-done), kind=kOutput, calls=%fused_computation.4 | convolution fusion | flops 1073872896 | bytes 6553600 | tf_op jit(solution)/shard_map/dot_general | solution.py:34
  187.1 0.1 reshape.27
  187.1 1.1 fusion.4
  188.2 0.0 all-gather.15.cloned.1.call-update
  188.2 69.1 %all-gather.9.cloned.1.call-done = bf16[4096,512]{1,0:T(8,128)(2,1)} async-done(((bf16[512,512]{1,0:T(8,128)(2,1)}), bf16[4096,512]{1,0:T(8,128)(2,1)}) %all-gather.9.cloned.1.call-update) | async-done | bytes 4194320 | tf_op jit(solution)/shard_map/all_gather | solution.py:29
  257.3 3.5 %multiply_convert_fusion.1 = bf16[256,512]{1,0:T(8,128)(2,1)S(1)} fusion(bf16[256,4096]{1,0:T(8,128)(2,1)S(1)} %bitcast.48, bf16[4096,512]{1,0:T(8,128)(2,1)} %all-gather.9.cloned.1.call-done), kind=kOutput, calls=%fused_computation.11 | convolution fusion | flops 1074397184 | bytes 6553600 | tf_op jit(solution)/shard_map/dot_general | solution.py:30
  260.8 0.1 reshape.25
  260.9 0.5 fusion.1
  261.4 69.6 %all-gather.15.cloned.1.call-done = f32[16,4,128,128]{3,2,1,0:T(8,128)} async-done(((f32[2,4,128,128]{3,2,1,0:T(8,128)}), f32[16,4,128,128]{3,2,1,0:T(8,128)}) %all-gather.15.cloned.1.call-update) | async-done | bytes 4194320 | tf_op jit(solution)/shard_map/all_gather | solution.py:11
  331.0 0.0 copy-start
  331.0 0.4 multiply_reduce_fusion
  331.4 0.3 copy-done
  331.7 0.1 fusion.3
  331.8 0.9 copy.17
  (4 shorter events, 0.1 us)
Async XLA Ops:
  6.5 27.7 %all-gather.7.cloned.1.call-start = ((), (), s32[]{:S(2)}) async-start(), calls=%async_computation | async-start | bytes 2621440 | tf_op jit(solution)/shard_map/all_gather | solution.py:25
  7.3 102.5 %all-gather.11.cloned.1.call-start = ((), (), s32[]{:S(2)}) async-start(), calls=%async_computation.2 | async-start | bytes 4718592 | tf_op jit(solution)/shard_map/all_gather | solution.py:31
  8.0 175.6 %all-gather.13.cloned.1.call-start = ((), (), s32[]{:S(2)}) async-start(), calls=%async_computation.3 | async-start | bytes 4718592 | tf_op jit(solution)/shard_map/all_gather | solution.py:33
  8.7 248.6 %all-gather.9.cloned.1.call-start = ((), (), s32[]{:S(2)}) async-start(), calls=%async_computation.1 | async-start | bytes 4718592 | tf_op jit(solution)/shard_map/all_gather | solution.py:29
  9.3 321.7 %all-gather.15.cloned.1.call-start = ((), (), s32[]{:S(2)}) async-start(), calls=%async_computation.4 | async-start | bytes 4718592 | tf_op jit(solution)/shard_map/all_gather | solution.py:11
  109.8 73.8 %copy-start.1 = (bf16[2,128,4096]{2,1,0:T(8,128)(2,1)S(1)}, bf16[2,128,4096]{2,1,0:T(8,128)(2,1)}, u32[]{:S(2)}) copy-start(bf16[2,128,4096]{2,1,0:T(8,128)(2,1)} %all-gather.7.cloned.1.call-done) | copy-start | bytes 6291460
  331.0 0.7 copy-start
Sparse Core Ops, SparseCore 0:
  8.9 25.2 all-gather.6
  36.4 73.3 all-gather.10
  111.9 71.6 all-gather.12
  185.6 71.6 all-gather.8
  259.3 71.6 all-gather.14
where the time goes:
time: 343 us; the launch traced here: 339 us
  waiting for transfers between devices  311 us (91%)
  between operations  13.2 us (4%)
  matrix products  13.1 us (4%)
    all_gather x1, waiting for transfers between devices, body(): key_full = lax.all_gather(w_key, 'ctx', axis=0, tiled=True)  75.6 us
    all_gather x1, waiting for transfers between devices, entering(): gathered = lax.all_gather(part, axis)  69.6 us
    all_gather x1, waiting for transfers between devices, body(): value_full = lax.all_gather(w_value, 'ctx', axis=0, tiled=True)  69.3 us
    all_gather x1, waiting for transfers between devices, body(): query_full = lax.all_gather(w_query, 'ctx', axis=0, tiled=True)  69.1 us
    all_gather x1, waiting for transfers between devices, body(): gathered = lax.all_gather(tokens, 'head', axis=2, tiled=True)  24.9 us
  transfers between devices with their start and end apart: 5, of which 5 were waited for; matrix products, arithmetic and copies ran while one was open for 4% of the time, Pallas kernels for 0%

commit v1 on v0

--- a/solution.py
+++ b/solution.py
@@ -1,9 +1,14 @@
+import functools
+
 import jax
 import jax.numpy as jnp
 from jax import lax
+from jax.experimental import pallas as pl
+from jax.experimental.pallas import tpu as pltpu
 from jax.sharding import PartitionSpec as P
 
 HD = 128
+MESH = pl.DeviceIdType.MESH
 
 
 def entering(part, axis, combine, identity):
@@ -21,7 +26,7 @@
     return earlier + later
 
 
-def body(tokens, w_query, w_key, w_value, norm_gain):
+def general_body(tokens, w_query, w_key, w_value, norm_gain):
     gathered = lax.all_gather(tokens, "head", axis=2, tiled=True)
     seq_count, span_len, model_dim = gathered.shape
     token_rows = gathered.reshape(seq_count * span_len, model_dim)
@@ -58,6 +63,218 @@
     return normed.transpose(0, 2, 1, 3).reshape(seq_count, span_len, features).astype(jnp.bfloat16)
 
 
+def silu(u):
+    return u / (1.0 + jnp.exp(-u))
+
+
+def mm(a, b):
+    return jnp.dot(a, b, preferred_element_type=jnp.float32)
+
+
+K, V, Q = 0, 1, 2
+
+
+def kernel(
+    tok_ref, wq_ref, wk_ref, wv_ref, gain_ref, out_ref,
+    atok, tok, wpeer, s1_out, s1_in, s2_out, s2_in, acc, proj, state, scan_out, scan_in, total,
+    a_send, a_recv, b_send, b_recv, c_send, c_recv, w_send, w_recv,
+    s1_send, s1_recv, s2_send, s2_recv, x_send, x_recv,
+):
+    c, h = lax.axis_index("ctx"), lax.axis_index("head")
+    y = lax.rem(c, 2)
+    zl = lax.rem(lax.div(c, 2), 2)
+    zh = lax.div(c, 4)
+    core = lax.rem(h, 2)
+    x = lax.div(h, 2)
+    c_y, c_l, c_h = c + 1 - 2 * y, c + 2 - 4 * zl, c + 4 - 8 * zh
+    c_hy = c_h + 1 - 2 * y
+    h_c, h_x = h + 1 - 2 * core, h + 2 - 4 * x
+    h_xc = h_x + 1 - 2 * core
+    weights = (wk_ref, wv_ref, wq_ref)
+    seqs, span, width = tok_ref.shape
+    half = width // 2
+    rows = seqs * span
+    heads = out_ref.shape[2] // HD
+
+    barrier = pltpu.get_barrier_semaphore()
+    peers = [(c, h_c), (c, h_x), (c, h_xc), (c_y, h), (c_h, h), (c_hy, h), (c_l, h)]
+    for peer in peers:
+        pl.semaphore_signal(barrier, inc=1, device_id=peer, device_id_type=MESH)
+    pl.semaphore_wait(barrier, len(peers))
+
+    def remote(src, dst, send, recv, peer):
+        return pltpu.make_async_remote_copy(
+            src_ref=src, dst_ref=dst, send_sem=send, recv_sem=recv, device_id=peer, device_id_type=MESH
+        )
+
+    pending = []
+
+    def go(copy):
+        copy.start()
+        pending.append(copy)
+        return copy
+
+    w_copies = [remote(weights[j], wpeer.at[j], w_send.at[j], w_recv.at[j], (c_l, h)) for j in range(3)]
+
+    a_copies = [
+        go(remote(tok_ref.at[1 - core], atok.at[h], a_send.at[0], a_recv.at[0], (c, h_c))),
+        go(remote(tok_ref.at[core], atok.at[h], a_send.at[1], a_recv.at[1], (c, h_x))),
+        go(remote(tok_ref.at[1 - core], atok.at[h], a_send.at[2], a_recv.at[2], (c, h_xc))),
+    ]
+    go(w_copies[K])
+    atok[h] = tok_ref[core]
+    for copy in a_copies:
+        copy.wait_recv()
+
+    def b_source(zd, yd):
+        return atok.at[pl.ds(2 * zd, 2), :, pl.ds(pl.multiple_of(yd * half, half), half)]
+
+    blk = 2 * zh + y
+    b_copies = [
+        go(remote(b_source(1 - zh, y), tok.at[blk, :, core], b_send.at[0], b_recv.at[0], (c_h, h))),
+        go(remote(b_source(1 - zh, 1 - y), tok.at[blk, :, core], b_send.at[1], b_recv.at[1], (c_hy, h))),
+        go(remote(b_source(zh, 1 - y), tok.at[blk, :, core], b_send.at[2], b_recv.at[2], (c_y, h))),
+    ]
+    go(w_copies[V])
+    go(w_copies[Q])
+    tok[blk, :, core] = b_source(zh, y)[...]
+
+    def share(n, place):
+        return go(remote(tok.at[place, :, core], tok.at[place, :, core], c_send.at[n], c_recv.at[n], (c, h_c)))
+
+    c_copies = [share(0, blk)]
+    b_copies[2].wait_recv()
+    c_copies.append(share(1, 2 * zh + 1 - y))
+    b_copies[0].wait_recv()
+    c_copies.append(share(2, 2 * (1 - zh) + y))
+    b_copies[1].wait_recv()
+    c_copies.append(share(3, 2 * (1 - zh) + 1 - y))
+    for copy in c_copies:
+        copy.wait_recv()
+
+    def partial(place, j):
+        mine = tok[place, zl].reshape(rows, half)
+        other = tok[place, 1 - zl].reshape(rows, half)
+        return mm(mine, weights[j][...]) + mm(other, wpeer[j])
+
+    s1_copies, s2_copies = {}, {}
+
+    def first(j):
+        w_copies[j].wait_recv()
+        for zd in range(2):
+            s1_out[j, zd] = partial(2 * zd + 1 - y, j).astype(jnp.bfloat16)
+            s1_copies[j, zd] = go(
+                remote(s1_out.at[j, zd], s1_in.at[j, zd], s1_send.at[2 * j + zd], s1_recv.at[2 * j + zd], (c_y, h))
+            )
+        acc[j, 0] = partial(2 * (1 - zh) + y, j)
+        acc[j, 1] = partial(2 * zh + y, j)
+
+    def second(j):
+        for zd in range(2):
+            s1_copies[j, zd].wait_recv()
+        s2_out[j] = (acc[j, 0] + s1_in[j, 1 - zh].astype(jnp.float32)).astype(jnp.bfloat16)
+        s2_copies[j] = go(remote(s2_out.at[j], s2_in.at[j], s2_send.at[j], s2_recv.at[j], (c_h, h)))
+        acc[j, 1] = acc[j, 1] + s1_in[j, zh].astype(jnp.float32)
+
+    def last(j):
+        s2_copies[j].wait_recv()
+        u = acc[j, 1] + s2_in[j].astype(jnp.float32)
+        if j != V:
+            u = silu(u)
+        proj[j] = u.astype(jnp.bfloat16)
+
+    def piece(j, s, n):
+        return proj[j, s * span:(s + 1) * span, n * HD:(n + 1) * HD]
+
+    pairs = [(s, n) for s in range(seqs) for n in range(heads)]
+
+    first(K)
+    first(V)
+    second(K)
+    first(Q)
+    second(V)
+    last(K)
+    last(V)
+    for i, (s, n) in enumerate(pairs):
+        state[i] = lax.dot_general(
+            piece(K, s, n), piece(V, s, n), (((0,), (0,)), ((), ())), preferred_element_type=jnp.float32
+        )
+
+    def send_states(step, peer):
+        scan_out[step] = state[...].astype(jnp.bfloat16)
+        return go(remote(scan_out.at[step], scan_in.at[step], x_send.at[step], x_recv.at[step], peer))
+
+    x0 = send_states(0, (c_y, h))
+    second(Q)
+    x0.wait_recv()
+    came = scan_in[0].astype(jnp.float32)
+    state[...] = state[...] + came
+    x1 = send_states(1, (c_l, h))
+    before = came * y.astype(jnp.float32)
+    x1.wait_recv()
+    came = scan_in[1].astype(jnp.float32)
+    state[...] = state[...] + came
+    x2 = send_states(2, (c_h, h))
+    state[...] = before + came * zl.astype(jnp.float32)
+
+    last(Q)
+    causal = lax.broadcasted_iota(jnp.int32, (span, span), 0) >= lax.broadcasted_iota(jnp.int32, (span, span), 1)
+    for i, (s, n) in enumerate(pairs):
+        scores = lax.dot_general(
+            piece(Q, s, n), piece(K, s, n), (((1,), (1,)), ((), ())), preferred_element_type=jnp.float32
+        )
+        masked = jnp.where(causal, scores, 0.0).astype(jnp.bfloat16)
+        total[i] = mm(masked, piece(V, s, n))
+
+    x2.wait_recv()
+    for i, (s, n) in enumerate(pairs):
+        prefix = state[i] + scan_in[2, i].astype(jnp.float32) * zh.astype(jnp.float32)
+        sums = total[i] + mm(piece(Q, s, n), prefix.astype(jnp.bfloat16))
+        scale_inv = lax.rsqrt(jnp.mean(sums * sums, axis=-1, keepdims=True) + 1e-06)
+        gain = gain_ref[:, n * HD:(n + 1) * HD]
+        out_ref[s, :, n * HD:(n + 1) * HD] = (sums * scale_inv * gain).astype(jnp.bfloat16)
+
+    for copy in pending:
+        copy.wait_send()
+
+
+def fused_body(tokens, w_query, w_key, w_value, norm_gain):
+    seqs, span, width = tokens.shape
+    depth, features = w_query.shape
+    rows, half, heads = seqs * span, width // 2, features // HD
+    bf, f32 = jnp.bfloat16, jnp.float32
+    dma = pltpu.SemaphoreType.DMA
+    return pl.pallas_call(
+        kernel,
+        out_shape=jax.ShapeDtypeStruct((seqs, span, features), bf),
+        in_specs=[pl.BlockSpec(memory_space=pltpu.VMEM)] * 5,
+        out_specs=pl.BlockSpec(memory_space=pltpu.VMEM),
+        scratch_shapes=[
+            pltpu.VMEM((4, span, width), bf),
+            pltpu.VMEM((4, 2, seqs, span, half), bf),
+            pltpu.VMEM((3, depth, features), bf),
+            pltpu.VMEM((3, 2, rows, features), bf),
+            pltpu.VMEM((3, 2, rows, features), bf),
+            pltpu.VMEM((3, rows, features), bf),
+            pltpu.VMEM((3, rows, features), bf),
+            pltpu.VMEM((3, 2, rows, features), f32),
+            pltpu.VMEM((3, rows, features), bf),
+            pltpu.VMEM((seqs * heads, HD, HD), f32),
+            pltpu.VMEM((3, seqs * heads, HD, HD), bf),
+            pltpu.VMEM((3, seqs * heads, HD, HD), bf),
+            pltpu.VMEM((seqs * heads, span, HD), f32),
+            dma((3,)), dma((3,)), dma((3,)), dma((3,)), dma((4,)), dma((4,)), dma((3,)), dma((3,)),
+            dma((6,)), dma((6,)), dma((3,)), dma((3,)), dma((3,)), dma((3,)),
+        ],
+        compiler_params=pltpu.CompilerParams(
+            collective_id=0, has_side_effects=True, vmem_limit_bytes=48 * 1024 * 1024
+        ),
+        cost_estimate=pl.CostEstimate(
+            flops=2 * rows * width * 4 * features * 3, bytes_accessed=3 * 2**20, transcendentals=0
+        ),
+    )(tokens, w_query, w_key, w_value, norm_gain.reshape(1, features))
+
+
 def solution(mesh):
     in_specs = (
         P(None, "ctx", "head"),
@@ -67,4 +284,6 @@
         P("head"),
     )
     out_specs = P(None, "ctx", "head")
+    fits = mesh.shape["ctx"] == 8 and mesh.shape["head"] == 4
+    body = fused_body if fits else general_body
     return jax.shard_map(body, mesh=mesh, in_specs=in_specs, out_specs=out_specs, check_vma=False)

time: 343 us -> 113 us (0.33)
  waiting for transfers between devices: 311 us -> 0 us
  Pallas kernels: 0 us -> 107 us
  between operations: 13.2 us -> 0.01 us
  matrix products: 13.1 us -> 0 us
  local copies, waits for them, and re-layouts: 1.57 us -> 5.55 us
    all_gather x5 -> x0, waiting for transfers between devices: 308 us -> none  [the longest x1 75.6 us: body(): key_full = lax.all_gather(w_key, 'ctx', axis=0, tiled=True)]
    pallas_call x0 -> x1, Pallas kernels: none -> 107 us  [fused_body(): pl.pallas_call(kernel, out_shape=jax.ShapeDtypeStruct((seqs, span, featur...]
    dot_general x6 -> x0, matrix products: 13.1 us -> none  [the longest x1 4.29 us: body(): key_sum = jnp.dot(token_rows, key_full, preferred_element_type=jnp.float32)]
    unnamed x4 -> x11, local copies, waits for them, and re-layouts: 0.3 us -> 5.55 us
  transfers between devices with their start and end apart: 5 -> 0, of which waited for: 5 -> 0; matrix products, arithmetic and copies ran while one was open for 4% -> 0% of each run, Pallas kernels for 0% -> 0%
where the time goes in v1:
time: 113 us
  Pallas kernels  107 us (95%)
  local copies, waits for them, and re-layouts  5.55 us (5%)
    pallas_call x1, Pallas kernels, fused_body(): pl.pallas_call(kernel, out_shape=jax.ShapeDtypeStruct((seqs, span, featur...  107 us
    unnamed x11, local copies, waits for them, and re-layouts  5.55 us

profile of v1, /device:TPU:0, one launch (start us, length us, event | category | flops | bytes accessed | tf_op | source)
XLA Modules:
  0.0 112.6 jit_solution(10965821286982898597)
XLA Ops:
  0.0 0.0 copy-start
  0.0 1.0 copy-done
  1.0 0.0 copy-start.1
  1.0 1.0 copy-done.1
  2.1 0.0 copy-start.2
  2.1 1.0 copy-done.2
  3.1 0.0 copy-start.3
  3.1 1.0 copy-done.3
  4.2 0.0 copy-start.4
  4.2 0.7 copy-done.4
  4.9 107.0 %shard_map.55 = bf16[2,128,512]{2,1,0:T(8,128)(2,1)S(1)} custom-call(bf16[2,128,1024]{2,1,0:T(8,128)(2,1)S(1)} %copy-done, bf16[512,512]{1,0:T(8,128)(2,1)S(1)} %copy-done.1, bf16[512,512]{1,0:T(8,128)(2,1)S(1)} %copy-done.2, bf16[512,512]{1,0:T(8,128)(2,1)S(1)} %copy-done.3, f32[1,512]{1,0:T(1,128)S(1)} %bitcast.1), custom_call_target="tpu_custom_call" | custom-call | flops 3221225472 | bytes 3145728 | tf_op jit(solution)/shard_map/pallas_call | solution.py:247
  111.9 0.7 copy.7
Async XLA Ops:
  0.0 1.0 copy-start
  1.0 1.0 copy-start.1
  2.1 1.0 copy-start.2
  3.1 1.0 copy-start.3
  4.2 0.7 copy-start.4

commit v2 on v1

--- a/solution.py
+++ b/solution.py
@@ -76,8 +76,8 @@
 
 def kernel(
     tok_ref, wq_ref, wk_ref, wv_ref, gain_ref, out_ref,
-    atok, tok, wpeer, s1_out, s1_in, s2_out, s2_in, acc, proj, state, scan_out, scan_in, total,
-    a_send, a_recv, b_send, b_recv, c_send, c_recv, w_send, w_recv,
+    atok, tok, wown, wpeer, s1_out, s1_in, s2_out, s2_in, acc, proj, state, scan_out, scan_in, total,
+    l_sem, a_send, a_recv, b_send, b_recv, c_send, c_recv, d_send, d_recv, w_send, w_recv,
     s1_send, s1_recv, s2_send, s2_recv, x_send, x_recv,
 ):
     c, h = lax.axis_index("ctx"), lax.axis_index("head")
@@ -93,8 +93,19 @@
     weights = (wk_ref, wv_ref, wq_ref)
     seqs, span, width = tok_ref.shape
     half = width // 2
+    part = span // 2
     rows = seqs * span
     heads = out_ref.shape[2] // HD
+
+    local = [pltpu.make_async_copy(weights[j], wown.at[j], l_sem.at[j]) for j in range(3)]
+    for copy in local:
+        copy.start()
+
+    def strip(r):
+        return pl.ds(pl.multiple_of(r * part, part), part)
+
+    own_piece = pltpu.make_async_copy(tok_ref.at[core, strip(x)], atok.at[h], l_sem.at[3])
+    own_piece.start()
 
     barrier = pltpu.get_barrier_semaphore()
     peers = [(c, h_c), (c, h_x), (c, h_xc), (c_y, h), (c_h, h), (c_hy, h), (c_l, h)]
@@ -102,79 +113,88 @@
         pl.semaphore_signal(barrier, inc=1, device_id=peer, device_id_type=MESH)
     pl.semaphore_wait(barrier, len(peers))
 
-    def remote(src, dst, send, recv, peer):
-        return pltpu.make_async_remote_copy(
+    pending = []
+
+    def go(src, dst, send, recv, peer):
+        copy = pltpu.make_async_remote_copy(
             src_ref=src, dst_ref=dst, send_sem=send, recv_sem=recv, device_id=peer, device_id_type=MESH
         )
-
-    pending = []
-
-    def go(copy):
         copy.start()
         pending.append(copy)
         return copy
 
-    w_copies = [remote(weights[j], wpeer.at[j], w_send.at[j], w_recv.at[j], (c_l, h)) for j in range(3)]
+    def a_go(n, s, r, peer):
+        return go(tok_ref.at[s, strip(r)], atok.at[h], a_send.at[n], a_recv.at[n], peer)
 
     a_copies = [
-        go(remote(tok_ref.at[1 - core], atok.at[h], a_send.at[0], a_recv.at[0], (c, h_c))),
-        go(remote(tok_ref.at[core], atok.at[h], a_send.at[1], a_recv.at[1], (c, h_x))),
-        go(remote(tok_ref.at[1 - core], atok.at[h], a_send.at[2], a_recv.at[2], (c, h_xc))),
+        a_go(0, core, 1 - x, (c, h_x)), a_go(1, 1 - core, 1 - x, (c, h_xc)), a_go(2, 1 - core, x, (c, h_c)),
     ]
-    go(w_copies[K])
-    atok[h] = tok_ref[core]
+
+    def w_go(j):
+        return go(weights[j], wpeer.at[j], w_send.at[j], w_recv.at[j], (c_l, h))
+
+    w_copies = [w_go(K)]
     for copy in a_copies:
         copy.wait_recv()
+    own_piece.wait()
 
     def b_source(zd, yd):
         return atok.at[pl.ds(2 * zd, 2), :, pl.ds(pl.multiple_of(yd * half, half), half)]
 
-    blk = 2 * zh + y
-    b_copies = [
-        go(remote(b_source(1 - zh, y), tok.at[blk, :, core], b_send.at[0], b_recv.at[0], (c_h, h))),
-        go(remote(b_source(1 - zh, 1 - y), tok.at[blk, :, core], b_send.at[1], b_recv.at[1], (c_hy, h))),
-        go(remote(b_source(zh, 1 - y), tok.at[blk, :, core], b_send.at[2], b_recv.at[2], (c_y, h))),
-    ]
-    go(w_copies[V])
-    go(w_copies[Q])
-    tok[blk, :, core] = b_source(zh, y)[...]
-
-    def share(n, place):
-        return go(remote(tok.at[place, :, core], tok.at[place, :, core], c_send.at[n], c_recv.at[n], (c, h_c)))
-
-    c_copies = [share(0, blk)]
-    b_copies[2].wait_recv()
-    c_copies.append(share(1, 2 * zh + 1 - y))
-    b_copies[0].wait_recv()
-    c_copies.append(share(2, 2 * (1 - zh) + y))
-    b_copies[1].wait_recv()
-    c_copies.append(share(3, 2 * (1 - zh) + 1 - y))
-    for copy in c_copies:
-        copy.wait_recv()
+    def piece_of(place):
+        return tok.at[place, :, core, strip(x)]
+
+    blk, blk_y, blk_h, blk_hy = 2 * zh + y, 2 * zh + 1 - y, 2 * (1 - zh) + y, 2 * (1 - zh) + 1 - y
+
+    def b_go(n, zd, yd, peer):
+        return go(b_source(zd, yd), piece_of(blk), b_send.at[n], b_recv.at[n], peer)
+
+    b_y = b_go(0, zh, 1 - y, (c_y, h))
+    b_h = b_go(1, 1 - zh, y, (c_h, h))
+    b_hy = b_go(2, 1 - zh, 1 - y, (c_hy, h))
+    w_copies += [w_go(V), w_go(Q)]
+    tok[blk, :, core, strip(x)] = b_source(zh, y)[...]
+
+    def c_go(n, place):
+        return go(piece_of(place), piece_of(place), c_send.at[n], c_recv.at[n], (c, h_x))
+
+    def d_go(n, place):
+        mine = tok.at[place, :, core]
+        return go(mine, mine, d_send.at[n], d_recv.at[n], (c, h_c))
+
+    def gather_pair(n, first_place, second_place, first_in, second_in):
+        if first_in is not None:
+            first_in.wait_recv()
+        c0 = c_go(n, first_place)
+        second_in.wait_recv()
+        c1 = c_go(n + 1, second_place)
+        c0.wait_recv()
+        d0 = d_go(n, first_place)
+        c1.wait_recv()
+        d1 = d_go(n + 1, second_place)
+        d0.wait_recv()
+        d1.wait_recv()
 
     def partial(place, j):
         mine = tok[place, zl].reshape(rows, half)
         other = tok[place, 1 - zl].reshape(rows, half)
-        return mm(mine, weights[j][...]) + mm(other, wpeer[j])
+        return mm(mine, wown[j]) + mm(other, wpeer[j])
 
     s1_copies, s2_copies = {}, {}
 
-    def first(j):
-        w_copies[j].wait_recv()
-        for zd in range(2):
-            s1_out[j, zd] = partial(2 * zd + 1 - y, j).astype(jnp.bfloat16)
-            s1_copies[j, zd] = go(
-                remote(s1_out.at[j, zd], s1_in.at[j, zd], s1_send.at[2 * j + zd], s1_recv.at[2 * j + zd], (c_y, h))
-            )
-        acc[j, 0] = partial(2 * (1 - zh) + y, j)
-        acc[j, 1] = partial(2 * zh + y, j)
+    def first(j, slot):
+        here, away = (blk, blk_y) if slot else (blk_h, blk_hy)
+        s1_out[j, slot] = partial(away, j).astype(jnp.bfloat16)
+        n = 2 * j + slot
+        s1_copies[j, slot] = go(s1_out.at[j, slot], s1_in.at[j, slot], s1_send.at[n], s1_recv.at[n], (c_y, h))
+        acc[j, slot] = partial(here, j)
 
     def second(j):
-        for zd in range(2):
-            s1_copies[j, zd].wait_recv()
-        s2_out[j] = (acc[j, 0] + s1_in[j, 1 - zh].astype(jnp.float32)).astype(jnp.bfloat16)
-        s2_copies[j] = go(remote(s2_out.at[j], s2_in.at[j], s2_send.at[j], s2_recv.at[j], (c_h, h)))
-        acc[j, 1] = acc[j, 1] + s1_in[j, zh].astype(jnp.float32)
+        s1_copies[j, 0].wait_recv()
+        s2_out[j] = (acc[j, 0] + s1_in[j, 0].astype(jnp.float32)).astype(jnp.bfloat16)
+        s2_copies[j] = go(s2_out.at[j], s2_in.at[j], s2_send.at[j], s2_recv.at[j], (c_h, h))
+        s1_copies[j, 1].wait_recv()
+        acc[j, 1] = acc[j, 1] + s1_in[j, 1].astype(jnp.float32)
 
     def last(j):
         s2_copies[j].wait_recv()
@@ -188,34 +208,51 @@
 
     pairs = [(s, n) for s in range(seqs) for n in range(heads)]
 
-    first(K)
-    first(V)
+    gather_pair(0, blk, blk_y, None, b_y)
+    for copy in local:
+        copy.wait()
+    w_copies[K].wait_recv()
+    first(K, 1)
+    gather_pair(2, blk_h, blk_hy, b_h, b_hy)
+    first(K, 0)
+    w_copies[V].wait_recv()
+    first(V, 0)
+    first(V, 1)
     second(K)
-    first(Q)
+    w_copies[Q].wait_recv()
+    first(Q, 0)
+    first(Q, 1)
     second(V)
     last(K)
     last(V)
-    for i, (s, n) in enumerate(pairs):
-        state[i] = lax.dot_general(
-            piece(K, s, n), piece(V, s, n), (((0,), (0,)), ((), ())), preferred_element_type=jnp.float32
-        )
-
-    def send_states(step, peer):
-        scan_out[step] = state[...].astype(jnp.bfloat16)
-        return go(remote(scan_out.at[step], scan_in.at[step], x_send.at[step], x_recv.at[step], peer))
-
-    x0 = send_states(0, (c_y, h))
+
+    def chunk(s):
+        return slice(s * heads, (s + 1) * heads)
+
+    def send_states(step, s, peer):
+        scan_out[step, chunk(s)] = state[chunk(s)].astype(jnp.bfloat16)
+        place = pl.ds(s * heads, heads)
+        n = step * seqs + s
+        return go(scan_out.at[step, place], scan_in.at[step, place], x_send.at[n], x_recv.at[n], peer)
+
+    x0, x1, x2 = [], [], []
+    for s in range(seqs):
+        for n in range(heads):
+            state[s * heads + n] = lax.dot_general(
+                piece(K, s, n), piece(V, s, n), (((0,), (0,)), ((), ())), preferred_element_type=jnp.float32
+            )
+        x0.append(send_states(0, s, (c_y, h)))
     second(Q)
-    x0.wait_recv()
-    came = scan_in[0].astype(jnp.float32)
-    state[...] = state[...] + came
-    x1 = send_states(1, (c_l, h))
-    before = came * y.astype(jnp.float32)
-    x1.wait_recv()
-    came = scan_in[1].astype(jnp.float32)
-    state[...] = state[...] + came
-    x2 = send_states(2, (c_h, h))
-    state[...] = before + came * zl.astype(jnp.float32)
+    for s in range(seqs):
+        x0[s].wait_recv()
+        state[chunk(s)] = state[chunk(s)] + scan_in[0, chunk(s)].astype(jnp.float32)
+        x1.append(send_states(1, s, (c_l, h)))
+    for s in range(seqs):
+        x1[s].wait_recv()
+        came = scan_in[1, chunk(s)].astype(jnp.float32)
+        state[chunk(s)] = state[chunk(s)] + came
+        x2.append(send_states(2, s, (c_h, h)))
+        state[chunk(s)] = came * zl.astype(jnp.float32) + scan_in[0, chunk(s)].astype(jnp.float32) * y.astype(jnp.float32)
 
     last(Q)
     causal = lax.broadcasted_iota(jnp.int32, (span, span), 0) >= lax.broadcasted_iota(jnp.int32, (span, span), 1)
@@ -226,8 +263,9 @@
         masked = jnp.where(causal, scores, 0.0).astype(jnp.bfloat16)
         total[i] = mm(masked, piece(V, s, n))
 
-    x2.wait_recv()
     for i, (s, n) in enumerate(pairs):
+        if n == 0:
+            x2[s].wait_recv()
         prefix = state[i] + scan_in[2, i].astype(jnp.float32) * zh.astype(jnp.float32)
         sums = total[i] + mm(piece(Q, s, n), prefix.astype(jnp.bfloat16))
         scale_inv = lax.rsqrt(jnp.mean(sums * sums, axis=-1, keepdims=True) + 1e-06)
@@ -244,14 +282,16 @@
     rows, half, heads = seqs * span, width // 2, features // HD
     bf, f32 = jnp.bfloat16, jnp.float32
     dma = pltpu.SemaphoreType.DMA
+    sems = [4, 3, 3, 3, 3, 4, 4, 4, 4, 3, 3, 6, 6, 3, 3, 3 * seqs, 3 * seqs]
     return pl.pallas_call(
         kernel,
         out_shape=jax.ShapeDtypeStruct((seqs, span, features), bf),
-        in_specs=[pl.BlockSpec(memory_space=pltpu.VMEM)] * 5,
+        in_specs=[pl.BlockSpec(memory_space=pltpu.HBM)] * 4 + [pl.BlockSpec(memory_space=pltpu.VMEM)],
         out_specs=pl.BlockSpec(memory_space=pltpu.VMEM),
         scratch_shapes=[
-            pltpu.VMEM((4, span, width), bf),
+            pltpu.VMEM((4, span // 2, width), bf),
             pltpu.VMEM((4, 2, seqs, span, half), bf),
+            pltpu.VMEM((3, depth, features), bf),
             pltpu.VMEM((3, depth, features), bf),
             pltpu.VMEM((3, 2, rows, features), bf),
             pltpu.VMEM((3, 2, rows, features), bf),
@@ -263,11 +303,9 @@
             pltpu.VMEM((3, seqs * heads, HD, HD), bf),
             pltpu.VMEM((3, seqs * heads, HD, HD), bf),
             pltpu.VMEM((seqs * heads, span, HD), f32),
-            dma((3,)), dma((3,)), dma((3,)), dma((3,)), dma((4,)), dma((4,)), dma((3,)), dma((3,)),
-            dma((6,)), dma((6,)), dma((3,)), dma((3,)), dma((3,)), dma((3,)),
-        ],
+        ] + [dma((n,)) for n in sems],
         compiler_params=pltpu.CompilerParams(
-            collective_id=0, has_side_effects=True, vmem_limit_bytes=48 * 1024 * 1024
+            collective_id=0, has_side_effects=True, vmem_limit_bytes=62 * 1024 * 1024
         ),
         cost_estimate=pl.CostEstimate(
             flops=2 * rows * width * 4 * features * 3, bytes_accessed=3 * 2**20, transcendentals=0

time: 113 us -> 93.5 us (0.83)
  Pallas kernels: 107 us -> 91.7 us
  local copies, waits for them, and re-layouts: 5.55 us -> 1.67 us
    pallas_call x1, Pallas kernels: 107 us -> 91.7 us  [fused_body(): pl.pallas_call(kernel, out_shape=jax.ShapeDtypeStruct((seqs, span, featur...]
    unnamed x11 -> x1, local copies, waits for them, and re-layouts: 5.55 us -> 1.67 us
where the time goes in v2:
time: 93.5 us; the launch traced here: 93.4 us
  Pallas kernels  91.7 us (98%)
  local copies, waits for them, and re-layouts  1.67 us (2%)
    pallas_call x1, Pallas kernels, fused_body(): pl.pallas_call(kernel, out_shape=jax.ShapeDtypeStruct((seqs, span, featur...  91.7 us

profile of v2, /device:TPU:0, one launch (start us, length us, event | category | flops | bytes accessed | tf_op | source)
XLA Modules:
  0.0 93.4 jit_solution(8388033139238163597)
XLA Ops:
  0.0 91.7 %shard_map.55 = bf16[2,128,512]{2,1,0:T(8,128)(2,1)} custom-call(bf16[2,128,1024]{2,1,0:T(8,128)(2,1)} %tok_ref.1, bf16[512,512]{1,0:T(8,128)(2,1)} %wq_ref.1, bf16[512,512]{1,0:T(8,128)(2,1)} %wk_ref.1, bf16[512,512]{1,0:T(8,128)(2,1)} %wv_ref.1, f32[1,512]{1,0:T(1,128)} %bitcast.1), custom_call_target="tpu_custom_call" | custom-call | flops 3221225472 | bytes 3145728 | tf_op jit(solution)/shard_map/pallas_call | solution.py:286
  91.7 1.7 %copy.7 = bf16[2,128,512]{2,1,0:T(8,128)(2,1)} copy(bf16[2,128,512]{2,1,0:T(8,128)(2,1)} %shard_map.55) | data formatting | bytes 524288

commit v3 on v2

v3 whole, which is shorter than its diff:
```python
import functools

import jax
import jax.numpy as jnp
from jax import lax
from jax.experimental import pallas as pl
from jax.experimental.pallas import tpu as pltpu
from jax.sharding import PartitionSpec as P

HD = 128
MESH = pl.DeviceIdType.MESH


def entering(part, axis, combine, identity):
    place = lax.axis_index(axis)
    gathered = lax.all_gather(part, axis)
    state = jnp.zeros_like(part) + jnp.asarray(identity, part.dtype)

    def one(hop, state):
        return combine(state, lax.dynamic_index_in_dim(gathered, hop, 0, False))

    return lax.fori_loop(0, place, one, state)


def add_states(earlier, later):
    return earlier + later


def general_body(tokens, w_query, w_key, w_value, norm_gain):
    gathered = lax.all_gather(tokens, "head", axis=2, tiled=True)
    seq_count, span_len, model_dim = gathered.shape
    token_rows = gathered.reshape(seq_count * span_len, model_dim)
    features = w_query.shape[1]
    query_full = lax.all_gather(w_query, "ctx", axis=0, tiled=True)
    query_sum = jnp.dot(token_rows, query_full, preferred_element_type=jnp.float32)
    key_full = lax.all_gather(w_key, "ctx", axis=0, tiled=True)
    key_sum = jnp.dot(token_rows, key_full, preferred_element_type=jnp.float32)
    value_full = lax.all_gather(w_value, "ctx", axis=0, tiled=True)
    value_sum = jnp.dot(token_rows, value_full, preferred_element_type=jnp.float32)
    head_count = features // HD

    def heads_first(projected):
        shaped = projected.astype(jnp.bfloat16).reshape(seq_count, span_len, head_count, HD)
        return shaped.transpose(0, 2, 1, 3)

    query = heads_first(jax.nn.silu(query_sum))
    key_all = heads_first(jax.nn.silu(key_sum))
    value_all = heads_first(value_sum)
    positions = jnp.arange(span_len)
    causal = positions[:, None] >= positions[None, :]
    scores = jnp.einsum("shtd,shud->shtu", query, key_all, preferred_element_type=jnp.float32)
    masked = jnp.where(causal, scores, 0.0).astype(jnp.bfloat16)
    local_out = jnp.einsum("shtu,shud->shtd", masked, value_all, preferred_element_type=jnp.float32)
    states = jnp.einsum("shud,shue->shde", key_all, value_all, preferred_element_type=jnp.float32)
    prefix = entering(states, "ctx", add_states, jnp.zeros_like(states))
    from_prefix = jnp.einsum(
        "shtd,shde->shte", query, prefix.astype(jnp.bfloat16), preferred_element_type=jnp.float32
    )
    total = local_out + from_prefix
    scale_inv = lax.rsqrt(jnp.mean(total * total, axis=-1, keepdims=True) + 1e-06)
    gain_view = norm_gain.reshape(1, head_count, 1, HD)
    normed = total * scale_inv * gain_view
    return normed.transpose(0, 2, 1, 3).reshape(seq_count, span_len, features).astype(jnp.bfloat16)


def silu(u):
    return u / (1.0 + jnp.exp(-u))


def mm(a, b):
    return jnp.dot(a, b, preferred_element_type=jnp.float32)


K, V, Q = 0, 1, 2


def kernel(
    tok_ref, wq_ref, wk_ref, wv_ref, gain_ref, out_ref,
    atok, tok, wown, wpeer, s1_out, s1_in, s2_out, s2_in, acc, proj, state, scan_out, scan_in, sum_out, sum_in,
    total, res_out, res_in,
    l_sem, a_send, a_recv, b_send, b_recv, e_send, e_recv, c_send, c_recv, d_send, d_recv, w_send, w_recv,
    s1_send, s1_recv, s2_send, s2_recv, x_send, x_recv, r_send, r_recv,
):
    c, h = lax.axis_index("ctx"), lax.axis_index("head")
    y = lax.rem(c, 2)
    zl = lax.rem(lax.div(c, 2), 2)
    zh = lax.div(c, 4)
    core = lax.rem(h, 2)
    x = lax.div(h, 2)
    c_y, c_l, c_h = c + 1 - 2 * y, c + 2 - 4 * zl, c + 4 - 8 * zh
    c_hy = c_h + 1 - 2 * y
    h_c, h_x = h + 1 - 2 * core, h + 2 - 4 * x
    h_xc = h_x + 1 - 2 * core
    weights = (wk_ref, wv_ref, wq_ref)
    seqs, span, width = tok_ref.shape
    half = width // 2
    part = span // 2
    rows = seqs * span
    cols = out_ref.shape[2] // 2
    heads = cols // HD

    def col_half(n):
        return pl.ds(pl.multiple_of(n * cols, cols), cols)

    local = [pltpu.make_async_copy(weights[j].at[:, col_half(zl)], wown.at[j], l_sem.at[j]) for j in range(3)]
    for copy in local:
        copy.start()

    def strip(r):
        return pl.ds(pl.multiple_of(r * part, part), part)

    own_piece = pltpu.make_async_copy(tok_ref.at[core, strip(x)], atok.at[h], l_sem.at[3])
    own_piece.start()

    barrier = pltpu.get_barrier_semaphore()
    peers = [(c, h_c), (c, h_x), (c, h_xc), (c_y, h), (c_h, h), (c_hy, h), (c_l, h)]
    for peer in peers:
        pl.semaphore_signal(barrier, inc=1, device_id=peer, device_id_type=MESH)
    pl.semaphore_wait(barrier, len(peers))

    pending = []

    def go(src, dst, send, recv, peer):
        copy = pltpu.make_async_remote_copy(
            src_ref=src, dst_ref=dst, send_sem=send, recv_sem=recv, device_id=peer, device_id_type=MESH
        )
        copy.start()
        pending.append(copy)
        return copy

    def a_go(n, s, r, peer):
        return go(tok_ref.at[s, strip(r)], atok.at[h], a_send.at[n], a_recv.at[n], peer)

    a_copies = [
        a_go(0, core, 1 - x, (c, h_x)), a_go(1, 1 - core, 1 - x, (c, h_xc)), a_go(2, 1 - core, x, (c, h_c)),
    ]

    def w_go(j):
        return go(weights[j].at[:, col_half(1 - zl)], wpeer.at[j], w_send.at[j], w_recv.at[j], (c_l, h))

    w_copies = [w_go(K)]
    for copy in a_copies:
        copy.wait_recv()
    own_piece.wait()

    def b_source(zd, yd):
        return atok.at[pl.ds(2 * zd, 2), :, pl.ds(pl.multiple_of(yd * half, half), half)]

    def piece_of(zp, place):
        return tok.at[zp, place, :, core, strip(x)]

    blk, blk_y, blk_h, blk_hy = 2 * zh + y, 2 * zh + 1 - y, 2 * (1 - zh) + y, 2 * (1 - zh) + 1 - y

    def b_go(n, zd, yd, peer):
        return go(b_source(zd, yd), piece_of(zl, blk), b_send.at[n], b_recv.at[n], peer)

    b_h = b_go(1, 1 - zh, y, (c_h, h))
    b_hy = b_go(2, 1 - zh, 1 - y, (c_hy, h))
    b_y = b_go(0, zh, 1 - y, (c_y, h))
    tok[zl, blk, :, core, strip(x)] = b_source(zh, y)[...]

    places = (blk, blk_y, blk_h, blk_hy)

    def e_go(n):
        mine = piece_of(zl, places[n])
        return go(mine, mine, e_send.at[n], e_recv.at[n], (c_l, h))

    def c_go(n):
        mine = piece_of(zl if n < 4 else 1 - zl, places[n % 4])
        return go(mine, mine, c_send.at[n], c_recv.at[n], (c, h_x))

    def d_go(n):
        mine = tok.at[zl if n < 4 else 1 - zl, places[n % 4], :, core]
        return go(mine, mine, d_send.at[n], d_recv.at[n], (c, h_c))

    def partial(zp, place, j):
        mine = tok[zp, place, zl].reshape(rows, half)
        other = tok[zp, place, 1 - zl].reshape(rows, half)
        return mm(mine, wown[j]) + mm(other, wpeer[j])

    s1_copies, s2_copies = {}, {}

    def first(j, slot):
        here, away = (blk, blk_y) if slot else (blk_h, blk_hy)
        for zp in range(2):
            s1_out[j, slot, zp] = partial(zp, away, j).astype(jnp.bfloat16)
        n = 2 * j + slot
        s1_copies[j, slot] = go(s1_out.at[j, slot], s1_in.at[j, slot], s1_send.at[n], s1_recv.at[n], (c_y, h))
        for zp in range(2):
            acc[j, slot, zp] = partial(zp, here, j)

    def second(j):
        s1_copies[j, 0].wait_recv()
        s2_out[j] = (acc[j, 0] + s1_in[j, 0].astype(jnp.float32)).astype(jnp.bfloat16)
        s2_copies[j] = go(s2_out.at[j], s2_in.at[j], s2_send.at[j], s2_recv.at[j], (c_h, h))

    def last(j):
        s1_copies[j, 1].wait_recv()
        s2_copies[j].wait_recv()
        u = acc[j, 1] + s1_in[j, 1].astype(jnp.float32) + s2_in[j].astype(jnp.float32)
        if j != V:
            u = silu(u)
        proj[j] = u.astype(jnp.bfloat16)

    def piece(j, zp, s, n):
        return proj[j, zp, s * span:(s + 1) * span, n * HD:(n + 1) * HD]

    pairs = [(s, n) for s in range(seqs) for n in range(heads)]

    e, cc, d = {}, {}, {}
    e[0], cc[0] = e_go(0), c_go(0)
    w_copies.append(w_go(V))
    b_y.wait_recv()
    e[1], cc[1] = e_go(1), c_go(1)
    w_copies.append(w_go(Q))
    for n in range(2):
        e[n].wait_recv()
        cc[4 + n] = c_go(4 + n)
    for n in range(2):
        cc[n].wait_recv()
        d[n] = d_go(n)
    for n, came in ((2, b_h), (3, b_hy)):
        came.wait_recv()
        e[n], cc[n] = e_go(n), c_go(n)
    for n in (4, 5):
        cc[n].wait_recv()
        d[n] = d_go(n)
    for n in (2, 3):
        e[n].wait_recv()
        cc[4 + n] = c_go(4 + n)
    for copy in local:
        copy.wait()
    w_copies[K].wait_recv()
    for n in (0, 1, 4, 5):
        d[n].wait_recv()
    first(K, 1)
    for n in (2, 3, 6, 7):
        cc[n].wait_recv()
        d[n] = d_go(n)
    w_copies[V].wait_recv()
    first(V, 1)
    for n in (2, 3, 6, 7):
        d[n].wait_recv()
    first(K, 0)
    first(V, 0)
    w_copies[Q].wait_recv()
    first(Q, 0)
    second(K)
    first(Q, 1)
    second(V)
    second(Q)
    last(K)
    last(V)

    for zp in range(2):
        for i, (s, n) in enumerate(pairs):
            state[zp, i] = lax.dot_general(
                piece(K, zp, s, n), piece(V, zp, s, n), (((0,), (0,)), ((), ())), preferred_element_type=jnp.float32
            )
    scan_out[...] = state[...].astype(jnp.bfloat16)
    x0 = go(scan_out, scan_in, x_send.at[0], x_recv.at[0], (c_y, h))

    causal = lax.broadcasted_iota(jnp.int32, (span, span), 0) >= lax.broadcasted_iota(jnp.int32, (span, span), 1)

    x0.wait_recv()
    both = state[0] + scan_in[0].astype(jnp.float32)
    sum_out[...] = (both + state[1] + scan_in[1].astype(jnp.float32)).astype(jnp.bfloat16)
    x1 = go(sum_out, sum_in, x_send.at[1], x_recv.at[1], (c_h, h))
    is_odd = y.astype(jnp.float32)
    state[0] = scan_in[0].astype(jnp.float32) * is_odd
    state[1] = both + scan_in[1].astype(jnp.float32) * is_odd

    last(Q)
    for zp in range(2):
        for i, (s, n) in enumerate(pairs):
            scores = lax.dot_general(
                piece(Q, zp, s, n), piece(K, zp, s, n), (((1,), (1,)), ((), ())), preferred_element_type=jnp.float32
            )
            masked = jnp.where(causal, scores, 0.0).astype(jnp.bfloat16)
            total[zp, i] = mm(masked, piece(V, zp, s, n))

    x1.wait_recv()

    def finish(zp, i, s, n):
        prefix = state[zp, i] + sum_in[i].astype(jnp.float32) * zh.astype(jnp.float32)
        sums = total[zp, i] + mm(piece(Q, zp, s, n), prefix.astype(jnp.bfloat16))
        scale_inv = lax.rsqrt(jnp.mean(sums * sums, axis=-1, keepdims=True) + 1e-06)
        gain = gain_ref[:, pl.ds(pl.multiple_of(zl * cols + n * HD, HD), HD)]
        return (sums * scale_inv * gain).astype(jnp.bfloat16)

    for i, (s, n) in enumerate(pairs):
        res_out[s, :, n * HD:(n + 1) * HD] = finish(1 - zl, i, s, n)
    res = go(res_out, res_in, r_send.at[0], r_recv.at[0], (c_l, h))
    for i, (s, n) in enumerate(pairs):
        out_ref[s, :, pl.ds(pl.multiple_of(zl * cols + n * HD, HD), HD)] = finish(zl, i, s, n)
    res.wait_recv()
    out_ref[:, :, col_half(1 - zl)] = res_in[...]

    for copy in pending:
        copy.wait_send()


def fused_body(tokens, w_query, w_key, w_value, norm_gain):
    seqs, span, width = tokens.shape
    depth, features = w_query.shape
    rows, half, cols = seqs * span, width // 2, features // 2
    states = seqs * cols // HD
    bf, f32 = jnp.bfloat16, jnp.float32
    dma = pltpu.SemaphoreType.DMA
    sems = [4, 3, 3, 3, 3, 4, 4, 8, 8, 8, 8, 3, 3, 6, 6, 3, 3, 2, 2, 1, 1]
    return pl.pallas_call(
        kernel,
        out_shape=jax.ShapeDtypeStruct((seqs, span, features), bf),
        in_specs=[pl.BlockSpec(memory_space=pltpu.HBM)] * 4 + [pl.BlockSpec(memory_space=pltpu.VMEM)],
        out_specs=pl.BlockSpec(memory_space=pltpu.VMEM),
        scratch_shapes=[
            pltpu.VMEM((4, span // 2, width), bf),
            pltpu.VMEM((2, 4, 2, seqs, span, half), bf),
            pltpu.VMEM((3, depth, cols), bf),
            pltpu.VMEM((3, depth, cols), bf),
            pltpu.VMEM((3, 2, 2, rows, cols), bf),
            pltpu.VMEM((3, 2, 2, rows, cols), bf),
            pltpu.VMEM((3, 2, rows, cols), bf),
            pltpu.VMEM((3, 2, rows, cols), bf),
            pltpu.VMEM((3, 2, 2, rows, cols), f32),
            pltpu.VMEM((3, 2, rows, cols), bf),
            pltpu.VMEM((2, states, HD, HD), f32),
            pltpu.VMEM((2, states, HD, HD), bf),
            pltpu.VMEM((2, states, HD, HD), bf),
            pltpu.VMEM((states, HD, HD), bf),
            pltpu.VMEM((states, HD, HD), bf),
            pltpu.VMEM((2, states, span, HD), f32),
            pltpu.VMEM((seqs, span, cols), bf),
            pltpu.VMEM((seqs, span, cols), bf),
        ] + [dma((n,)) for n in sems],
        compiler_params=pltpu.CompilerParams(
            collective_id=0, has_side_effects=True, vmem_limit_bytes=62 * 1024 * 1024
        ),
        cost_estimate=pl.CostEstimate(
            flops=2 * rows * width * 4 * features * 3, bytes_accessed=3 * 2**20, transcendentals=0
        ),
    )(tokens, w_query, w_key, w_value, norm_gain.reshape(1, features))


def solution(mesh):
    in_specs = (
        P(None, "ctx", "head"),
        P("ctx", "head"),
        P("ctx", "head"),
        P("ctx", "head"),
        P("head"),
    )
    out_specs = P(None, "ctx", "head")
    fits = mesh.shape["ctx"] == 8 and mesh.shape["head"] == 4
    body = fused_body if fits else general_body
    return jax.shard_map(body, mesh=mesh, in_specs=in_specs, out_specs=out_specs, check_vma=False)
```

time: 93.5 us -> 113 us (1.21)
  Pallas kernels: 91.7 us -> 111 us
    pallas_call x1, Pallas kernels: 91.7 us -> 111 us  [fused_body(): pl.pallas_call(kernel, out_shape=jax.ShapeDtypeStruct((seqs, span, featur...]
where the time goes in v3:
time: 113 us
  Pallas kernels  111 us (98%)
  local copies, waits for them, and re-layouts  1.67 us (1%)
    pallas_call x1, Pallas kernels, fused_body(): pl.pallas_call(kernel, out_shape=jax.ShapeDtypeStruct((seqs, span, featur...  111 us

profile of v3, /device:TPU:0, one launch (start us, length us, event | category | flops | bytes accessed | tf_op | source)
XLA Modules:
  0.0 113.2 jit_solution(1439281245354332441)
XLA Ops:
  0.0 111.5 %shard_map.55 = bf16[2,128,512]{2,1,0:T(8,128)(2,1)} custom-call(bf16[2,128,1024]{2,1,0:T(8,128)(2,1)} %tok_ref.1, bf16[512,512]{1,0:T(8,128)(2,1)} %wq_ref.1, bf16[512,512]{1,0:T(8,128)(2,1)} %wk_ref.1, bf16[512,512]{1,0:T(8,128)(2,1)} %wv_ref.1, f32[1,512]{1,0:T(1,128)} %bitcast.1), custom_call_target="tpu_custom_call" | custom-call | flops 3221225472 | bytes 3145728 | tf_op jit(solution)/shard_map/pallas_call | solution.py:311
  111.5 1.7 %copy.7 = bf16[2,128,512]{2,1,0:T(8,128)(2,1)} copy(bf16[2,128,512]{2,1,0:T(8,128)(2,1)} %shard_map.55) | data formatting | bytes 524288

commit v4 on v2

--- a/solution.py
+++ b/solution.py
@@ -95,16 +95,20 @@
     half = width // 2
     part = span // 2
     rows = seqs * span
-    heads = out_ref.shape[2] // HD
-
-    local = [pltpu.make_async_copy(weights[j], wown.at[j], l_sem.at[j]) for j in range(3)]
-    for copy in local:
-        copy.start()
+    cols = out_ref.shape[2] // 2
+    heads = cols // HD
+
+    chunks = [(K, 0), (V, 0), (K, 1), (V, 1), (Q, 0), (Q, 1)]
+    local = {}
+    for j, g in chunks:
+        source = weights[j].at[:, g * cols:(g + 1) * cols]
+        local[j, g] = pltpu.make_async_copy(source, wown.at[j, g], l_sem.at[2 * j + g])
+        local[j, g].start()
 
     def strip(r):
         return pl.ds(pl.multiple_of(r * part, part), part)
 
-    own_piece = pltpu.make_async_copy(tok_ref.at[core, strip(x)], atok.at[h], l_sem.at[3])
+    own_piece = pltpu.make_async_copy(tok_ref.at[core, strip(x)], atok.at[h], l_sem.at[6])
     own_piece.start()
 
     barrier = pltpu.get_barrier_semaphore()
@@ -130,10 +134,11 @@
         a_go(0, core, 1 - x, (c, h_x)), a_go(1, 1 - core, 1 - x, (c, h_xc)), a_go(2, 1 - core, x, (c, h_c)),
     ]
 
-    def w_go(j):
-        return go(weights[j], wpeer.at[j], w_send.at[j], w_recv.at[j], (c_l, h))
-
-    w_copies = [w_go(K)]
+    def w_go(j, g):
+        local[j, g].wait()
+        return go(wown.at[j, g], wpeer.at[j, g], w_send.at[2 * j + g], w_recv.at[2 * j + g], (c_l, h))
+
+    w_copies = {at: w_go(*at) for at in chunks[:2]}
     for copy in a_copies:
         copy.wait_recv()
     own_piece.wait()
@@ -152,7 +157,7 @@
     b_y = b_go(0, zh, 1 - y, (c_y, h))
     b_h = b_go(1, 1 - zh, y, (c_h, h))
     b_hy = b_go(2, 1 - zh, 1 - y, (c_hy, h))
-    w_copies += [w_go(V), w_go(Q)]
+    w_copies.update({at: w_go(*at) for at in chunks[2:]})
     tok[blk, :, core, strip(x)] = b_source(zh, y)[...]
 
     def c_go(n, place):
@@ -175,102 +180,123 @@
         d0.wait_recv()
         d1.wait_recv()
 
-    def partial(place, j):
+    def partial(place, j, g):
         mine = tok[place, zl].reshape(rows, half)
         other = tok[place, 1 - zl].reshape(rows, half)
-        return mm(mine, wown[j]) + mm(other, wpeer[j])
+        return mm(mine, wown[j, g]) + mm(other, wpeer[j, g])
 
     s1_copies, s2_copies = {}, {}
-
-    def first(j, slot):
+    arrived = set()
+
+    def first(j, g, slot):
+        if (j, g) not in arrived:
+            w_copies[j, g].wait_recv()
+            arrived.add((j, g))
         here, away = (blk, blk_y) if slot else (blk_h, blk_hy)
-        s1_out[j, slot] = partial(away, j).astype(jnp.bfloat16)
-        n = 2 * j + slot
-        s1_copies[j, slot] = go(s1_out.at[j, slot], s1_in.at[j, slot], s1_send.at[n], s1_recv.at[n], (c_y, h))
-        acc[j, slot] = partial(here, j)
-
-    def second(j):
-        s1_copies[j, 0].wait_recv()
-        s2_out[j] = (acc[j, 0] + s1_in[j, 0].astype(jnp.float32)).astype(jnp.bfloat16)
-        s2_copies[j] = go(s2_out.at[j], s2_in.at[j], s2_send.at[j], s2_recv.at[j], (c_h, h))
-        s1_copies[j, 1].wait_recv()
-        acc[j, 1] = acc[j, 1] + s1_in[j, 1].astype(jnp.float32)
-
-    def last(j):
-        s2_copies[j].wait_recv()
-        u = acc[j, 1] + s2_in[j].astype(jnp.float32)
+        s1_out[j, g, slot] = partial(away, j, g).astype(jnp.bfloat16)
+        n = 4 * j + 2 * g + slot
+        s1_copies[j, g, slot] = go(
+            s1_out.at[j, g, slot], s1_in.at[j, g, slot], s1_send.at[n], s1_recv.at[n], (c_y, h)
+        )
+        acc[j, g, slot] = partial(here, j, g)
+
+    def second(j, g):
+        s1_copies[j, g, 0].wait_recv()
+        s2_out[j, g] = (acc[j, g, 0] + s1_in[j, g, 0].astype(jnp.float32)).astype(jnp.bfloat16)
+        n = 2 * j + g
+        s2_copies[j, g] = go(s2_out.at[j, g], s2_in.at[j, g], s2_send.at[n], s2_recv.at[n], (c_h, h))
+
+    def last(j, g):
+        s1_copies[j, g, 1].wait_recv()
+        s2_copies[j, g].wait_recv()
+        u = acc[j, g, 1] + s1_in[j, g, 1].astype(jnp.float32) + s2_in[j, g].astype(jnp.float32)
         if j != V:
             u = silu(u)
-        proj[j] = u.astype(jnp.bfloat16)
-
-    def piece(j, s, n):
-        return proj[j, s * span:(s + 1) * span, n * HD:(n + 1) * HD]
+        proj[j, g] = u.astype(jnp.bfloat16)
+
+    def piece(j, g, s, n):
+        return proj[j, g, s * span:(s + 1) * span, n * HD:(n + 1) * HD]
 
     pairs = [(s, n) for s in range(seqs) for n in range(heads)]
 
+    def send_states(step, g, peer):
+        scan_out[step, g] = state[g].astype(jnp.bfloat16)
+        n = step * 2 + g
+        return go(scan_out.at[step, g], scan_in.at[step, g], x_send.at[n], x_recv.at[n], peer)
+
+    x0, x1, x2 = {}, {}, {}
+
+    def states(g):
+        last(K, g)
+        last(V, g)
+        for i, (s, n) in enumerate(pairs):
+            state[g, i] = lax.dot_general(
+                piece(K, g, s, n), piece(V, g, s, n), (((0,), (0,)), ((), ())), preferred_element_type=jnp.float32
+            )
+        x0[g] = send_states(0, g, (c_y, h))
+
+    def scan_y(g):
+        x0[g].wait_recv()
+        state[g] = state[g] + scan_in[0, g].astype(jnp.float32)
+        x1[g] = send_states(1, g, (c_l, h))
+
+    def scan_l(g):
+        x1[g].wait_recv()
+        came = scan_in[1, g].astype(jnp.float32)
+        state[g] = state[g] + came
+        x2[g] = send_states(2, g, (c_h, h))
+        state[g] = came * zl.astype(jnp.float32) + scan_in[0, g].astype(jnp.float32) * y.astype(jnp.float32)
+
+    causal = lax.broadcasted_iota(jnp.int32, (span, span), 0) >= lax.broadcasted_iota(jnp.int32, (span, span), 1)
+
+    def within(g):
+        last(Q, g)
+        for i, (s, n) in enumerate(pairs):
+            scores = lax.dot_general(
+                piece(Q, g, s, n), piece(K, g, s, n), (((1,), (1,)), ((), ())), preferred_element_type=jnp.float32
+            )
+            masked = jnp.where(causal, scores, 0.0).astype(jnp.bfloat16)
+            total[g, i] = mm(masked, piece(V, g, s, n))
+
+    def finish(g):
+        x2[g].wait_recv()
+        for i, (s, n) in enumerate(pairs):
+            prefix = state[g, i] + scan_in[2, g, i].astype(jnp.float32) * zh.astype(jnp.float32)
+            sums = total[g, i] + mm(piece(Q, g, s, n), prefix.astype(jnp.bfloat16))
+            scale_inv = lax.rsqrt(jnp.mean(sums * sums, axis=-1, keepdims=True) + 1e-06)
+            at = slice(g * cols + n * HD, g * cols + (n + 1) * HD)
+            out_ref[s, :, at] = (sums * scale_inv * gain_ref[:, at]).astype(jnp.bfloat16)
+
     gather_pair(0, blk, blk_y, None, b_y)
-    for copy in local:
-        copy.wait()
-    w_copies[K].wait_recv()
-    first(K, 1)
+    first(K, 0, 1)
+    first(V, 0, 1)
     gather_pair(2, blk_h, blk_hy, b_h, b_hy)
-    first(K, 0)
-    w_copies[V].wait_recv()
-    first(V, 0)
-    first(V, 1)
-    second(K)
-    w_copies[Q].wait_recv()
-    first(Q, 0)
-    first(Q, 1)
-    second(V)
-    last(K)
-    last(V)
-
-    def chunk(s):
-        return slice(s * heads, (s + 1) * heads)
-
-    def send_states(step, s, peer):
-        scan_out[step, chunk(s)] = state[chunk(s)].astype(jnp.bfloat16)
-        place = pl.ds(s * heads, heads)
-        n = step * seqs + s
-        return go(scan_out.at[step, place], scan_in.at[step, place], x_send.at[n], x_recv.at[n], peer)
-
-    x0, x1, x2 = [], [], []
-    for s in range(seqs):
-        for n in range(heads):
-            state[s * heads + n] = lax.dot_general(
-                piece(K, s, n), piece(V, s, n), (((0,), (0,)), ((), ())), preferred_element_type=jnp.float32
-            )
-        x0.append(send_states(0, s, (c_y, h)))
-    second(Q)
-    for s in range(seqs):
-        x0[s].wait_recv()
-        state[chunk(s)] = state[chunk(s)] + scan_in[0, chunk(s)].astype(jnp.float32)
-        x1.append(send_states(1, s, (c_l, h)))
-    for s in range(seqs):
-        x1[s].wait_recv()
-        came = scan_in[1, chunk(s)].astype(jnp.float32)
-        state[chunk(s)] = state[chunk(s)] + came
-        x2.append(send_states(2, s, (c_h, h)))
-        state[chunk(s)] = came * zl.astype(jnp.float32) + scan_in[0, chunk(s)].astype(jnp.float32) * y.astype(jnp.float32)
-
-    last(Q)
-    causal = lax.broadcasted_iota(jnp.int32, (span, span), 0) >= lax.broadcasted_iota(jnp.int32, (span, span), 1)
-    for i, (s, n) in enumerate(pairs):
-        scores = lax.dot_general(
-            piece(Q, s, n), piece(K, s, n), (((1,), (1,)), ((), ())), preferred_element_type=jnp.float32
-        )
-        masked = jnp.where(causal, scores, 0.0).astype(jnp.bfloat16)
-        total[i] = mm(masked, piece(V, s, n))
-
-    for i, (s, n) in enumerate(pairs):
-        if n == 0:
-            x2[s].wait_recv()
-        prefix = state[i] + scan_in[2, i].astype(jnp.float32) * zh.astype(jnp.float32)
-        sums = total[i] + mm(piece(Q, s, n), prefix.astype(jnp.bfloat16))
-        scale_inv = lax.rsqrt(jnp.mean(sums * sums, axis=-1, keepdims=True) + 1e-06)
-        gain = gain_ref[:, n * HD:(n + 1) * HD]
-        out_ref[s, :, n * HD:(n + 1) * HD] = (sums * scale_inv * gain).astype(jnp.bfloat16)
+    first(K, 0, 0)
+    first(V, 0, 0)
+    first(K, 1, 0)
+    first(V, 1, 0)
+    second(K, 0)
+    second(V, 0)
+    first(K, 1, 1)
+    first(V, 1, 1)
+    second(K, 1)
+    second(V, 1)
+    first(Q, 0, 0)
+    states(0)
+    first(Q, 0, 1)
+    scan_y(0)
+    first(Q, 1, 0)
+    second(Q, 0)
+    states(1)
+    first(Q, 1, 1)
+    scan_l(0)
+    second(Q, 1)
+    scan_y(1)
+    within(0)
+    scan_l(1)
+    within(1)
+    finish(0)
+    finish(1)
 
     for copy in pending:
         copy.wait_send()
@@ -279,10 +305,11 @@
 def fused_body(tokens, w_query, w_key, w_value, norm_gain):
     seqs, span, width = tokens.shape
     depth, features = w_query.shape
-    rows, half, heads = seqs * span, width // 2, features // HD
+    rows, half, cols = seqs * span, width // 2, features // 2
+    states = seqs * cols // HD
     bf, f32 = jnp.bfloat16, jnp.float32
     dma = pltpu.SemaphoreType.DMA
-    sems = [4, 3, 3, 3, 3, 4, 4, 4, 4, 3, 3, 6, 6, 3, 3, 3 * seqs, 3 * seqs]
+    sems = [7, 3, 3, 3, 3, 4, 4, 4, 4, 6, 6, 12, 12, 6, 6, 6, 6]
     return pl.pallas_call(
         kernel,
         out_shape=jax.ShapeDtypeStruct((seqs, span, features), bf),
@@ -291,18 +318,18 @@
         scratch_shapes=[
             pltpu.VMEM((4, span // 2, width), bf),
             pltpu.VMEM((4, 2, seqs, span, half), bf),
-            pltpu.VMEM((3, depth, features), bf),
-            pltpu.VMEM((3, depth, features), bf),
-            pltpu.VMEM((3, 2, rows, features), bf),
-            pltpu.VMEM((3, 2, rows, features), bf),
-            pltpu.VMEM((3, rows, features), bf),
-            pltpu.VMEM((3, rows, features), bf),
-            pltpu.VMEM((3, 2, rows, features), f32),
-            pltpu.VMEM((3, rows, features), bf),
-            pltpu.VMEM((seqs * heads, HD, HD), f32),
-            pltpu.VMEM((3, seqs * heads, HD, HD), bf),
-            pltpu.VMEM((3, seqs * heads, HD, HD), bf),
-            pltpu.VMEM((seqs * heads, span, HD), f32),
+            pltpu.VMEM((3, 2, depth, cols), bf),
+            pltpu.VMEM((3, 2, depth, cols), bf),
+            pltpu.VMEM((3, 2, 2, rows, cols), bf),
+            pltpu.VMEM((3, 2, 2, rows, cols), bf),
+            pltpu.VMEM((3, 2, rows, cols), bf),
+            pltpu.VMEM((3, 2, rows, cols), bf),
+            pltpu.VMEM((3, 2, 2, rows, cols), f32),
+            pltpu.VMEM((3, 2, rows, cols), bf),
+            pltpu.VMEM((2, states, HD, HD), f32),
+            pltpu.VMEM((3, 2, states, HD, HD), bf),
+            pltpu.VMEM((3, 2, states, HD, HD), bf),
+            pltpu.VMEM((2, states, span, HD), f32),
         ] + [dma((n,)) for n in sems],
         compiler_params=pltpu.CompilerParams(
             collective_id=0, has_side_effects=True, vmem_limit_bytes=62 * 1024 * 1024

time: 93.5 us -> 90.1 us (0.964)
  Pallas kernels: 91.7 us -> 88.2 us
    pallas_call x1, Pallas kernels: 91.7 us -> 88.2 us  [fused_body(): pl.pallas_call(kernel, out_shape=jax.ShapeDtypeStruct((seqs, span, featur...]
where the time goes in v4:
time: 90.1 us; the launch traced here: 89.9 us
  Pallas kernels  88.2 us (98%)
  local copies, waits for them, and re-layouts  1.67 us (2%)
    pallas_call x1, Pallas kernels, fused_body(): pl.pallas_call(kernel, out_shape=jax.ShapeDtypeStruct((seqs, span, featur...  88.2 us

profile of v4, /device:TPU:0, one launch (start us, length us, event | category | flops | bytes accessed | tf_op | source)
XLA Modules:
  0.0 89.9 jit_solution(2988883033470424679)
XLA Ops:
  0.0 88.2 %shard_map.55 = bf16[2,128,512]{2,1,0:T(8,128)(2,1)} custom-call(bf16[2,128,1024]{2,1,0:T(8,128)(2,1)} %tok_ref.1, bf16[512,512]{1,0:T(8,128)(2,1)} %wq_ref.1, bf16[512,512]{1,0:T(8,128)(2,1)} %wk_ref.1, bf16[512,512]{1,0:T(8,128)(2,1)} %wv_ref.1, f32[1,512]{1,0:T(1,128)} %bitcast.1), custom_call_target="tpu_custom_call" | custom-call | flops 3221225472 | bytes 3145728 | tf_op jit(solution)/shard_map/pallas_call | solution.py:313
  88.3 1.7 %copy.7 = bf16[2,128,512]{2,1,0:T(8,128)(2,1)} copy(bf16[2,128,512]{2,1,0:T(8,128)(2,1)} %shard_map.55) | data formatting | bytes 524288

commit v5 on v4

--- a/solution.py
+++ b/solution.py
@@ -138,7 +138,7 @@
         local[j, g].wait()
         return go(wown.at[j, g], wpeer.at[j, g], w_send.at[2 * j + g], w_recv.at[2 * j + g], (c_l, h))
 
-    w_copies = {at: w_go(*at) for at in chunks[:2]}
+    w_copies = {at: w_go(*at) for at in chunks[:1]}
     for copy in a_copies:
         copy.wait_recv()
     own_piece.wait()
@@ -157,7 +157,7 @@
     b_y = b_go(0, zh, 1 - y, (c_y, h))
     b_h = b_go(1, 1 - zh, y, (c_h, h))
     b_hy = b_go(2, 1 - zh, 1 - y, (c_hy, h))
-    w_copies.update({at: w_go(*at) for at in chunks[2:]})
+    w_copies[V, 0] = w_go(V, 0)
     tok[blk, :, core, strip(x)] = b_source(zh, y)[...]
 
     def c_go(n, place):
@@ -167,12 +167,14 @@
         mine = tok.at[place, :, core]
         return go(mine, mine, d_send.at[n], d_recv.at[n], (c, h_c))
 
-    def gather_pair(n, first_place, second_place, first_in, second_in):
+    def gather_pair(n, first_place, second_place, first_in, second_in, then=()):
         if first_in is not None:
             first_in.wait_recv()
         c0 = c_go(n, first_place)
         second_in.wait_recv()
         c1 = c_go(n + 1, second_place)
+        for at in then:
+            w_copies[at] = w_go(*at)
         c0.wait_recv()
         d0 = d_go(n, first_place)
         c1.wait_recv()
@@ -270,7 +272,7 @@
     gather_pair(0, blk, blk_y, None, b_y)
     first(K, 0, 1)
     first(V, 0, 1)
-    gather_pair(2, blk_h, blk_hy, b_h, b_hy)
+    gather_pair(2, blk_h, blk_hy, b_h, b_hy, chunks[2:])
     first(K, 0, 0)
     first(V, 0, 0)
     first(K, 1, 0)

time: 90.1 us -> 92.5 us (1.027)
  Pallas kernels: 88.2 us -> 90.6 us
    pallas_call x1, Pallas kernels: 88.2 us -> 90.6 us  [fused_body(): pl.pallas_call(kernel, out_shape=jax.ShapeDtypeStruct((seqs, span, featur...]
where the time goes in v5:
time: 92.5 us; the launch traced here: 92.3 us
  Pallas kernels  90.6 us (98%)
  local copies, waits for them, and re-layouts  1.67 us (2%)
    pallas_call x1, Pallas kernels, fused_body(): pl.pallas_call(kernel, out_shape=jax.ShapeDtypeStruct((seqs, span, featur...  90.6 us

profile of v5, /device:TPU:0, one launch (start us, length us, event | category | flops | bytes accessed | tf_op | source)
XLA Modules:
  0.0 92.3 jit_solution(15291195294518281676)
XLA Ops:
  0.0 90.6 %shard_map.55 = bf16[2,128,512]{2,1,0:T(8,128)(2,1)} custom-call(bf16[2,128,1024]{2,1,0:T(8,128)(2,1)} %tok_ref.1, bf16[512,512]{1,0:T(8,128)(2,1)} %wq_ref.1, bf16[512,512]{1,0:T(8,128)(2,1)} %wk_ref.1, bf16[512,512]{1,0:T(8,128)(2,1)} %wv_ref.1, f32[1,512]{1,0:T(1,128)} %bitcast.1), custom_call_target="tpu_custom_call" | custom-call | flops 3221225472 | bytes 3145728 | tf_op jit(solution)/shard_map/pallas_call | solution.py:315
  90.6 1.7 %copy.7 = bf16[2,128,512]{2,1,0:T(8,128)(2,1)} copy(bf16[2,128,512]{2,1,0:T(8,128)(2,1)} %shard_map.55) | data formatting | bytes 524288

commit v6 on v4

--- a/solution.py
+++ b/solution.py
@@ -88,6 +88,8 @@
     x = lax.div(h, 2)
     c_y, c_l, c_h = c + 1 - 2 * y, c + 2 - 4 * zl, c + 4 - 8 * zh
     c_hy = c_h + 1 - 2 * y
+    z = 2 * zh + zl
+    c_m = 6 - 2 * z + y
     h_c, h_x = h + 1 - 2 * core, h + 2 - 4 * x
     h_xc = h_x + 1 - 2 * core
     weights = (wk_ref, wv_ref, wq_ref)
@@ -112,7 +114,7 @@
     own_piece.start()
 
     barrier = pltpu.get_barrier_semaphore()
-    peers = [(c, h_c), (c, h_x), (c, h_xc), (c_y, h), (c_h, h), (c_hy, h), (c_l, h)]
+    peers = [(c, h_c), (c, h_x), (c, h_xc), (c_y, h), (c_h, h), (c_hy, h), (c_l, h), (c_m, h)]
     for peer in peers:
         pl.semaphore_signal(barrier, inc=1, device_id=peer, device_id_type=MESH)
     pl.semaphore_wait(barrier, len(peers))
@@ -224,7 +226,7 @@
         n = step * 2 + g
         return go(scan_out.at[step, g], scan_in.at[step, g], x_send.at[n], x_recv.at[n], peer)
 
-    x0, x1, x2 = {}, {}, {}
+    x0 = {}
 
     def states(g):
         last(K, g)
@@ -235,17 +237,33 @@
             )
         x0[g] = send_states(0, g, (c_y, h))
 
+    def up(g):
+        return pltpu.make_async_remote_copy(
+            src_ref=scan_out.at[1, g], dst_ref=scan_in.at[1, g], send_sem=x_send.at[2 + g],
+            recv_sem=x_recv.at[2 + g], device_id=(lax.rem(c + 2, 8), h), device_id_type=MESH,
+        )
+
     def scan_y(g):
         x0[g].wait_recv()
         state[g] = state[g] + scan_in[0, g].astype(jnp.float32)
-        x1[g] = send_states(1, g, (c_l, h))
-
-    def scan_l(g):
-        x1[g].wait_recv()
-        came = scan_in[1, g].astype(jnp.float32)
-        state[g] = state[g] + came
-        x2[g] = send_states(2, g, (c_h, h))
-        state[g] = came * zl.astype(jnp.float32) + scan_in[0, g].astype(jnp.float32) * y.astype(jnp.float32)
+
+        @pl.when(z == 0)
+        def _():
+            scan_in[1, g] = jnp.zeros(scan_in.shape[2:], scan_in.dtype)
+            scan_out[1, g] = state[g].astype(jnp.bfloat16)
+            up(g).start()
+
+    def scan_z(g):
+        @pl.when(z > 0)
+        def _():
+            up(g).wait_recv()
+
+            @pl.when(z < 3)
+            def _():
+                scan_out[1, g] = (state[g] + scan_in[1, g].astype(jnp.float32)).astype(jnp.bfloat16)
+                up(g).start()
+
+        state[g] = scan_in[1, g].astype(jnp.float32) + scan_in[0, g].astype(jnp.float32) * y.astype(jnp.float32)
 
     causal = lax.broadcasted_iota(jnp.int32, (span, span), 0) >= lax.broadcasted_iota(jnp.int32, (span, span), 1)
 
@@ -259,10 +277,8 @@
             total[g, i] = mm(masked, piece(V, g, s, n))
 
     def finish(g):
-        x2[g].wait_recv()
         for i, (s, n) in enumerate(pairs):
-            prefix = state[g, i] + scan_in[2, g, i].astype(jnp.float32) * zh.astype(jnp.float32)
-            sums = total[g, i] + mm(piece(Q, g, s, n), prefix.astype(jnp.bfloat16))
+            sums = total[g, i] + mm(piece(Q, g, s, n), state[g, i].astype(jnp.bfloat16))
             scale_inv = lax.rsqrt(jnp.mean(sums * sums, axis=-1, keepdims=True) + 1e-06)
             at = slice(g * cols + n * HD, g * cols + (n + 1) * HD)
             out_ref[s, :, at] = (sums * scale_inv * gain_ref[:, at]).astype(jnp.bfloat16)
@@ -289,14 +305,19 @@
     second(Q, 0)
     states(1)
     first(Q, 1, 1)
-    scan_l(0)
     second(Q, 1)
     scan_y(1)
+    scan_z(0)
     within(0)
-    scan_l(1)
+    scan_z(1)
+    finish(0)
     within(1)
-    finish(0)
     finish(1)
+
+    @pl.when(z < 3)
+    def _():
+        for g in range(2):
+            up(g).wait_send()
 
     for copy in pending:
         copy.wait_send()
@@ -309,7 +330,7 @@
     states = seqs * cols // HD
     bf, f32 = jnp.bfloat16, jnp.float32
     dma = pltpu.SemaphoreType.DMA
-    sems = [7, 3, 3, 3, 3, 4, 4, 4, 4, 6, 6, 12, 12, 6, 6, 6, 6]
+    sems = [7, 3, 3, 3, 3, 4, 4, 4, 4, 6, 6, 12, 12, 6, 6, 4, 4]
     return pl.pallas_call(
         kernel,
         out_shape=jax.ShapeDtypeStruct((seqs, span, features), bf),
@@ -327,8 +348,8 @@
             pltpu.VMEM((3, 2, 2, rows, cols), f32),
             pltpu.VMEM((3, 2, rows, cols), bf),
             pltpu.VMEM((2, states, HD, HD), f32),
-            pltpu.VMEM((3, 2, states, HD, HD), bf),
-            pltpu.VMEM((3, 2, states, HD, HD), bf),
+            pltpu.VMEM((2, 2, states, HD, HD), bf),
+            pltpu.VMEM((2, 2, states, HD, HD), bf),
             pltpu.VMEM((2, states, span, HD), f32),
         ] + [dma((n,)) for n in sems],
         compiler_params=pltpu.CompilerParams(

time: 90.1 us -> 87.5 us (0.971)
  the two profiles are of different devices: /device:TPU:0 before, /device:TPU:24 now
where the time goes in v6:
time: 87.5 us; the launch traced here: 87.4 us
  Pallas kernels  85.7 us (98%)
  local copies, waits for them, and re-layouts  1.67 us (2%)
    pallas_call x1, Pallas kernels, fused_body(): pl.pallas_call(kernel, out_shape=jax.ShapeDtypeStruct((seqs, span, featur...  85.7 us

profile of v6, /device:TPU:24, one launch (start us, length us, event | category | flops | bytes accessed | tf_op | source)
XLA Modules:
  0.0 87.4 jit_solution(11009451390913709172)
XLA Ops:
  0.0 85.7 %shard_map.55 = bf16[2,128,512]{2,1,0:T(8,128)(2,1)} custom-call(bf16[2,128,1024]{2,1,0:T(8,128)(2,1)} %tok_ref.1, bf16[512,512]{1,0:T(8,128)(2,1)} %wq_ref.1, bf16[512,512]{1,0:T(8,128)(2,1)} %wk_ref.1, bf16[512,512]{1,0:T(8,128)(2,1)} %wv_ref.1, f32[1,512]{1,0:T(1,128)} %bitcast.1), custom_call_target="tpu_custom_call" | custom-call | flops 3221225472 | bytes 3145728 | tf_op jit(solution)/shard_map/pallas_call | solution.py:334
  85.7 1.7 %copy.7 = bf16[2,128,512]{2,1,0:T(8,128)(2,1)} copy(bf16[2,128,512]{2,1,0:T(8,128)(2,1)} %shard_map.55) | data formatting | bytes 524288

commit v7 on v6

--- a/solution.py
+++ b/solution.py
@@ -76,8 +76,8 @@
 
 def kernel(
     tok_ref, wq_ref, wk_ref, wv_ref, gain_ref, out_ref,
-    atok, tok, wown, wpeer, s1_out, s1_in, s2_out, s2_in, acc, proj, state, scan_out, scan_in, total,
-    l_sem, a_send, a_recv, b_send, b_recv, c_send, c_recv, d_send, d_recv, w_send, w_recv,
+    tok, wown, wpeer, s1_out, s1_in, s2_out, s2_in, acc, proj, state, scan_out, scan_in, total,
+    l_sem, b_send, b_recv, c_send, c_recv, d_send, d_recv, w_send, w_recv,
     s1_send, s1_recv, s2_send, s2_recv, x_send, x_recv,
 ):
     c, h = lax.axis_index("ctx"), lax.axis_index("head")
@@ -110,11 +110,9 @@
     def strip(r):
         return pl.ds(pl.multiple_of(r * part, part), part)
 
-    own_piece = pltpu.make_async_copy(tok_ref.at[core, strip(x)], atok.at[h], l_sem.at[6])
-    own_piece.start()
-
     barrier = pltpu.get_barrier_semaphore()
-    peers = [(c, h_c), (c, h_x), (c, h_xc), (c_y, h), (c_h, h), (c_hy, h), (c_l, h), (c_m, h)]
+    same_zl = [(where, to) for where in (c, c_y, c_h, c_hy) for to in (h, h_c, h_x, h_xc)]
+    peers = same_zl[1:] + [(c_l, h), (c_m, h)]
     for peer in peers:
         pl.semaphore_signal(barrier, inc=1, device_id=peer, device_id_type=MESH)
     pl.semaphore_wait(barrier, len(peers))
@@ -129,38 +127,68 @@
         pending.append(copy)
         return copy
 
-    def a_go(n, s, r, peer):
-        return go(tok_ref.at[s, strip(r)], atok.at[h], a_send.at[n], a_recv.at[n], peer)
-
-    a_copies = [
-        a_go(0, core, 1 - x, (c, h_x)), a_go(1, 1 - core, 1 - x, (c, h_xc)), a_go(2, 1 - core, x, (c, h_c)),
-    ]
-
     def w_go(j, g):
         local[j, g].wait()
         return go(wown.at[j, g], wpeer.at[j, g], w_send.at[2 * j + g], w_recv.at[2 * j + g], (c_l, h))
 
-    w_copies = {at: w_go(*at) for at in chunks[:2]}
-    for copy in a_copies:
-        copy.wait_recv()
-    own_piece.wait()
-
-    def b_source(zd, yd):
-        return atok.at[pl.ds(2 * zd, 2), :, pl.ds(pl.multiple_of(yd * half, half), half)]
+    w_copies = {at: w_go(*at) for at in chunks[:1]}
+    blk, blk_y, blk_h, blk_hy = 2 * zh + y, 2 * zh + 1 - y, 2 * (1 - zh) + y, 2 * (1 - zh) + 1 - y
+    at_home = x == zh
+
+    def b_copy(n):
+        yd, s, r = (1 - y if n & 4 else y), (1 - core if n & 1 else core), (1 - x if n & 2 else x)
+        src = tok_ref.at[s, strip(r), pl.ds(pl.multiple_of(yd * half, half), half)]
+        dst = tok.at[blk, core, s, strip(r)]
+        if n == 0:
+            stays = pltpu.make_async_copy(src, dst, l_sem.at[6])
+        else:
+            stays = None
+        goes = pltpu.make_async_remote_copy(
+            src_ref=src, dst_ref=dst, send_sem=b_send.at[n], recv_sem=b_recv.at[2 * blk + core],
+            device_id=(4 * x + 2 * zl + yd, 2 * r + s), device_id_type=MESH,
+        )
+        return stays, goes
+
+    for n in (7, 6, 5, 4, 3, 2, 1):
+        goes = b_copy(n)[1]
+        goes.start()
+        pending.append(goes)
+    stays, goes = b_copy(0)
+
+    @pl.when(at_home)
+    def _():
+        stays.start()
+
+    @pl.when(jnp.logical_not(at_home))
+    def _():
+        goes.start()
+
+    def b_wait(place, own=False):
+        for l in range(2):
+            dst = tok.at[place, l, core, strip(x)]
+            came = pltpu.make_async_remote_copy(
+                src_ref=dst, dst_ref=dst, send_sem=b_send.at[0], recv_sem=b_recv.at[2 * place + l],
+                device_id=(c, h_c), device_id_type=MESH,
+            )
+            if not own:
+                came.wait_recv()
+                continue
+            mine = jnp.logical_and(at_home, core == l)
+
+            @pl.when(mine)
+            def _():
+                stays.wait()
+
+            @pl.when(jnp.logical_not(mine))
+            def _():
+                came.wait_recv()
+
+    w_copies[V, 0] = w_go(V, 0)
 
     def piece_of(place):
         return tok.at[place, :, core, strip(x)]
 
-    blk, blk_y, blk_h, blk_hy = 2 * zh + y, 2 * zh + 1 - y, 2 * (1 - zh) + y, 2 * (1 - zh) + 1 - y
-
-    def b_go(n, zd, yd, peer):
-        return go(b_source(zd, yd), piece_of(blk), b_send.at[n], b_recv.at[n], peer)
-
-    b_y = b_go(0, zh, 1 - y, (c_y, h))
-    b_h = b_go(1, 1 - zh, y, (c_h, h))
-    b_hy = b_go(2, 1 - zh, 1 - y, (c_hy, h))
     w_copies.update({at: w_go(*at) for at in chunks[2:]})
-    tok[blk, :, core, strip(x)] = b_source(zh, y)[...]
 
     def c_go(n, place):
         return go(piece_of(place), piece_of(place), c_send.at[n], c_recv.at[n], (c, h_x))
@@ -169,11 +197,10 @@
         mine = tok.at[place, :, core]
         return go(mine, mine, d_send.at[n], d_recv.at[n], (c, h_c))
 
-    def gather_pair(n, first_place, second_place, first_in, second_in):
-        if first_in is not None:
-            first_in.wait_recv()
+    def gather_pair(n, first_place, second_place):
+        b_wait(first_place, n == 0)
         c0 = c_go(n, first_place)
-        second_in.wait_recv()
+        b_wait(second_place)
         c1 = c_go(n + 1, second_place)
         c0.wait_recv()
         d0 = d_go(n, first_place)
@@ -283,10 +310,10 @@
             at = slice(g * cols + n * HD, g * cols + (n + 1) * HD)
             out_ref[s, :, at] = (sums * scale_inv * gain_ref[:, at]).astype(jnp.bfloat16)
 
-    gather_pair(0, blk, blk_y, None, b_y)
+    gather_pair(0, blk, blk_y)
     first(K, 0, 1)
     first(V, 0, 1)
-    gather_pair(2, blk_h, blk_hy, b_h, b_hy)
+    gather_pair(2, blk_h, blk_hy)
     first(K, 0, 0)
     first(V, 0, 0)
     first(K, 1, 0)
@@ -319,6 +346,10 @@
         for g in range(2):
             up(g).wait_send()
 
+    @pl.when(jnp.logical_not(at_home))
+    def _():
+        goes.wait_send()
+
     for copy in pending:
         copy.wait_send()
 
@@ -330,14 +361,13 @@
     states = seqs * cols // HD
     bf, f32 = jnp.bfloat16, jnp.float32
     dma = pltpu.SemaphoreType.DMA
-    sems = [7, 3, 3, 3, 3, 4, 4, 4, 4, 6, 6, 12, 12, 6, 6, 4, 4]
+    sems = [7, 8, 8, 4, 4, 4, 4, 6, 6, 12, 12, 6, 6, 4, 4]
     return pl.pallas_call(
         kernel,
         out_shape=jax.ShapeDtypeStruct((seqs, span, features), bf),
         in_specs=[pl.BlockSpec(memory_space=pltpu.HBM)] * 4 + [pl.BlockSpec(memory_space=pltpu.VMEM)],
         out_specs=pl.BlockSpec(memory_space=pltpu.VMEM),
         scratch_shapes=[
-            pltpu.VMEM((4, span // 2, width), bf),
             pltpu.VMEM((4, 2, seqs, span, half), bf),
             pltpu.VMEM((3, 2, depth, cols), bf),
             pltpu.VMEM((3, 2, depth, cols), bf),
@@ -353,7 +383,7 @@
             pltpu.VMEM((2, states, span, HD), f32),
         ] + [dma((n,)) for n in sems],
         compiler_params=pltpu.CompilerParams(
-            collective_id=0, has_side_effects=True, vmem_limit_bytes=62 * 1024 * 1024
+            collective_id=0, has_side_effects=True, vmem_limit_bytes=107 * 512 * 1024
         ),
         cost_estimate=pl.CostEstimate(
             flops=2 * rows * width * 4 * features * 3, bytes_accessed=3 * 2**20, transcendentals=0

time: 87.5 us -> 89.8 us (1.026)
  the two profiles are of different devices: /device:TPU:24 before, /device:TPU:26 now
where the time goes in v7:
time: 89.8 us; the launch traced here: 89.6 us
  Pallas kernels  88.2 us (98%)
  local copies, waits for them, and re-layouts  1.39 us (2%)
    pallas_call x1, Pallas kernels, fused_body(): pl.pallas_call(kernel, out_shape=jax.ShapeDtypeStruct((seqs, span, featur...  88.2 us

profile of v7, /device:TPU:26, one launch (start us, length us, event | category | flops | bytes accessed | tf_op | source)
XLA Modules:
  0.0 89.6 jit_solution(13194437683161266315)
XLA Ops:
  0.0 0.0 copy-start
  0.0 0.7 copy-done
  0.7 88.2 %shard_map.55 = bf16[2,128,512]{2,1,0:T(8,128)(2,1)S(1)} custom-call(bf16[2,128,1024]{2,1,0:T(8,128)(2,1)} %tok_ref.1, bf16[512,512]{1,0:T(8,128)(2,1)} %wq_ref.1, bf16[512,512]{1,0:T(8,128)(2,1)} %wk_ref.1, bf16[512,512]{1,0:T(8,128)(2,1)} %wv_ref.1, f32[1,512]{1,0:T(1,128)S(1)} %bitcast.1), custom_call_target="tpu_custom_call" | custom-call | flops 3221225472 | bytes 3145728 | tf_op jit(solution)/shard_map/pallas_call | solution.py:365
  88.9 0.7 copy.7
Async XLA Ops:
  0.0 0.7 copy-start

commit v8 on v6

--- a/solution.py
+++ b/solution.py
@@ -353,7 +353,7 @@
             pltpu.VMEM((2, states, span, HD), f32),
         ] + [dma((n,)) for n in sems],
         compiler_params=pltpu.CompilerParams(
-            collective_id=0, has_side_effects=True, vmem_limit_bytes=62 * 1024 * 1024
+            collective_id=0, has_side_effects=True, vmem_limit_bytes=107 * 512 * 1024
         ),
         cost_estimate=pl.CostEstimate(
             flops=2 * rows * width * 4 * features * 3, bytes_accessed=3 * 2**20, transcendentals=0

time: 87.5 us -> 85.9 us (0.982)
  Pallas kernels: 85.7 us -> 84.3 us
    pallas_call x1, Pallas kernels: 85.7 us -> 84.3 us  [fused_body(): pl.pallas_call(kernel, out_shape=jax.ShapeDtypeStruct((seqs, span, featur...]
where the time goes in v8:
time: 85.9 us; the launch traced here: 85.7 us
  Pallas kernels  84.3 us (98%)
  local copies, waits for them, and re-layouts  1.39 us (2%)
    pallas_call x1, Pallas kernels, fused_body(): pl.pallas_call(kernel, out_shape=jax.ShapeDtypeStruct((seqs, span, featur...  84.3 us

profile of v8, /device:TPU:24, one launch (start us, length us, event | category | flops | bytes accessed | tf_op | source)
XLA Modules:
  0.0 85.7 jit_solution(12160451352800491973)
XLA Ops:
  0.0 0.0 copy-start
  0.0 0.7 copy-done
  0.7 84.3 %shard_map.55 = bf16[2,128,512]{2,1,0:T(8,128)(2,1)S(1)} custom-call(bf16[2,128,1024]{2,1,0:T(8,128)(2,1)} %tok_ref.1, bf16[512,512]{1,0:T(8,128)(2,1)} %wq_ref.1, bf16[512,512]{1,0:T(8,128)(2,1)} %wk_ref.1, bf16[512,512]{1,0:T(8,128)(2,1)} %wv_ref.1, f32[1,512]{1,0:T(1,128)S(1)} %bitcast.1), custom_call_target="tpu_custom_call" | custom-call | flops 3221225472 | bytes 3145728 | tf_op jit(solution)/shard_map/pallas_call | solution.py:334
  85.0 0.7 copy.7
Async XLA Ops:
  0.0 0.7 copy-start
